TPU v7x, 512 devices: a whole 4x4x16 slice. The times are simulated.
512 devices in a mesh: seq: 128 (over y, z, core), tp: 4 (over x).
Axes of the slice: x: 4, y: 4, z: 16, core: 2. Of those that a mesh axis runs over, the one named last changes fastest.
Arguments:
- layer_input: bfloat16 [16384, 1600], P(('seq', 'tp')), may hold values from -6 to 6
- out_grad: bfloat16 [16384, 1600], P(('seq', 'tp')), may hold values from -2.5 to 2.5
- w_in: bfloat16 [1600, 1600], P('tp'), may hold values from -0.15625 to 0.15625
- w_gate: bfloat16 [1600, 1600], P('tp'), may hold values from -0.15625 to 0.15625
- w_out: bfloat16 [1600, 1600], P('tp'), may hold values from -0.15625 to 0.15625
- b_proj: bfloat16 [16, 16384], P(None, 'seq'), may hold values from -3 to 3
- c_proj: bfloat16 [16, 16384], P(None, 'seq'), may hold values from -3 to 3
- log_decay: bfloat16 [25, 16384], P(None, 'seq'), may hold values from -1 to 0
- d_skip: float32 [1600], P('tp'), may hold values from 0.5 to 1.5
- entry_state: float32 [16, 1600], P(None, 'tp'), may hold values from -6 to 6
- doc_start: int32 [16384], P('seq'), may hold values 0 or 1
Outputs:
- input_grad: bfloat16 [16384, 1600], P(('seq', 'tp'))
- b_grad: float32 [16, 16384], P(None, 'seq')
- c_grad: float32 [16, 16384], P(None, 'seq')
All inputs are finite; a program needn't handle non-finite values. No bound on the sum of `doc_start` on one device may be relied on, other than what follows from the above.
Results may differ from a plain program's by a relative error of at most 0.0065.
Values may be sent and summed in bfloat16 or wider, within the bound.
A program may use at most 128 MiB of HBM per device.

v0:
```python
import math

import jax
import jax.numpy as jnp
from jax import lax
from jax.sharding import PartitionSpec as P

HDIM = 64
UNIT = 2
BLK = 128


FULL_PRECISION = lax.Precision.HIGHEST


def silu_slope(values):
    logistic = jax.nn.sigmoid(values)
    return logistic * (1.0 + values * (1.0 - logistic))


def combine_pairs(earlier, later_pair):
    return (earlier[0] * later_pair[0], later_pair[0][..., None, :] * earlier[1] + later_pair[1])


def split_blocks(values):
    leading = values.shape[:-1]
    block_count = values.shape[-1] // BLK
    return jnp.moveaxis(values.reshape(leading + (block_count, BLK)), -2, 0)


def join_blocks(values):
    moved_axes = jnp.moveaxis(values, 0, -2)
    return moved_axes.reshape(moved_axes.shape[:-2] + (moved_axes.shape[-2] * BLK,))


def prepare(x_rows, y_grads, log_rows, marks, b_rows, c_rows):
    log_blocks = split_blocks(log_rows)
    mark_blocks = split_blocks(marks)
    cumulative = jnp.cumsum(log_blocks, axis=-1)
    counts = jnp.cumsum(mark_blocks, axis=-1)
    fresh_rows = (counts == 0).astype(jnp.float32)
    inside = (counts == counts[:, -1:]).astype(jnp.float32)
    totals = cumulative[..., -1]
    scales = jnp.where(mark_blocks[:, None, :] == 1, 1.0, jnp.sqrt(-jnp.expm1(2.0 * log_blocks)))
    scaled = split_blocks(x_rows).astype(jnp.float32) * scales
    gradient = split_blocks(y_grads).astype(jnp.float32)
    b_blocks = split_blocks(b_rows).astype(jnp.float32)
    c_blocks = split_blocks(c_rows).astype(jnp.float32)
    carry_in = jnp.exp(cumulative) * fresh_rows[:, None, :]
    carry_out = jnp.exp(totals[..., None] - cumulative) * inside[:, None, :]
    factor = jnp.exp(totals) * fresh_rows[:, -1:]
    state_part = jnp.einsum("bnq,bmq->bnm", b_blocks, scaled * carry_out, precision=FULL_PRECISION)
    grad_part = jnp.einsum("bnq,bmq->bnm", c_blocks, gradient * carry_in, precision=FULL_PRECISION)
    return (
        cumulative,
        counts,
        scaled,
        gradient,
        b_blocks,
        c_blocks,
        carry_in,
        carry_out,
        scales,
        factor,
        state_part,
        grad_part,
    )


def block_scans(parts):
    factor, state_part, grad_part = (parts[9], parts[10], parts[11])
    inc_factor, inc_state = lax.associative_scan(combine_pairs, (factor, state_part))
    rev_factor, rev_grad = lax.associative_scan(combine_pairs, (factor, grad_part), reverse=True)
    unit_rows = jnp.ones_like(factor[:1])
    empty_rows = jnp.zeros_like(state_part[:1])
    before = (
        jnp.concatenate([unit_rows, inc_factor[:-1]], axis=0),
        jnp.concatenate([empty_rows, inc_state[:-1]], axis=0),
    )
    behind = (
        jnp.concatenate([rev_factor[1:], unit_rows], axis=0),
        jnp.concatenate([rev_grad[1:], empty_rows], axis=0),
    )
    return (before, behind, (inc_factor[-1], inc_state[-1], rev_grad[0]))


def block_pass(pieces):
    cumulative, counts, scaled, gradient, b_blk, c_blk, carry_in, carry_out, state_in, grad_in = (
        pieces
    )
    centre = cumulative[:, BLK // 2][:, None]
    rising = jnp.exp(cumulative - centre)
    falling = jnp.exp(centre - cumulative)
    upper_rows = gradient * rising
    lower_rows = scaled * falling
    positions = jnp.arange(BLK)
    causal_mask = (positions[:, None] >= positions[None, :]) & (counts[:, None] == counts[None, :])
    crossed = jnp.where(causal_mask, jnp.dot(c_blk.T, b_blk, precision=FULL_PRECISION), 0.0)
    weight = jnp.where(
        causal_mask, jnp.dot(upper_rows.T, lower_rows, precision=FULL_PRECISION), 0.0
    )
    ssm_part = rising * jnp.dot(
        lower_rows, crossed.T, precision=FULL_PRECISION
    ) + carry_in * jnp.dot(state_in.T, c_blk, precision=FULL_PRECISION)
    x_part = falling * jnp.dot(upper_rows, crossed, precision=FULL_PRECISION) + carry_out * jnp.dot(
        grad_in.T, b_blk, precision=FULL_PRECISION
    )
    c_part = jnp.dot(b_blk, weight.T, precision=FULL_PRECISION) + jnp.dot(
        state_in, gradient * carry_in, precision=FULL_PRECISION
    )
    b_part = jnp.dot(c_blk, weight, precision=FULL_PRECISION) + jnp.dot(
        grad_in, scaled * carry_out, precision=FULL_PRECISION
    )
    return (ssm_part, x_part, b_part, c_part)


def group_leading(values, group_size):
    return values.reshape((values.shape[0] // group_size, group_size) + values.shape[1:])


def ungroup_leading(values):
    return values.reshape((values.shape[0] * values.shape[1],) + values.shape[2:])


def finish(parts, edges, state_dev, grad_dev, skip_gain, x_rows, y_grads):
    before, behind = (edges[0], edges[1])
    state_in = before[0][:, None, :] * state_dev[None] + before[1]
    grad_in = behind[0][:, None, :] * grad_dev[None] + behind[1]
    pieces = parts[:8] + (state_in, grad_in)
    block_count = parts[0].shape[0]
    group_size = math.gcd(block_count, 16)
    grouped = tuple((group_leading(values, group_size) for values in pieces))
    results = lax.map(jax.vmap(block_pass), grouped)
    ssm_blocks, x_blocks, b_blocks, c_blocks = tuple(
        (ungroup_leading(values) for values in results)
    )
    ssm_out = (join_blocks(ssm_blocks) + skip_gain[:, None] * x_rows.astype(jnp.float32)).astype(
        jnp.bfloat16
    )
    x_grad = (
        join_blocks(x_blocks * parts[8]) + skip_gain[:, None] * y_grads.astype(jnp.float32)
    ).astype(jnp.bfloat16)
    return (ssm_out, x_grad, join_blocks(b_blocks), join_blocks(c_blocks))


def shards(
    layer_input,
    out_grad,
    w_in,
    w_gate,
    w_out,
    b_proj,
    c_proj,
    log_decay,
    d_skip,
    entry_state,
    doc_start,
):
    rows_in, rows_grad = (
        lax.all_gather(layer_input, "tp", axis=0, tiled=True),
        lax.all_gather(out_grad, "tp", axis=0, tiled=True),
    )
    contract = (((1,), (1,)), ((), ()))
    pre_act = lax.dot_general(w_in, rows_in, contract, preferred_element_type=jnp.float32)
    gate_act = lax.dot_general(w_gate, rows_in, contract, preferred_element_type=jnp.float32)
    mix_grad = lax.dot_general(w_out, rows_grad, contract, preferred_element_type=jnp.float32)
    x_rows = jax.nn.silu(pre_act).astype(jnp.bfloat16)
    y_grads = (mix_grad * jax.nn.silu(gate_act)).astype(jnp.bfloat16)
    channels, tokens_here = x_rows.shape
    head_count = log_decay.shape[0]
    head_of = (lax.axis_index("tp") * channels + jnp.arange(channels)) // HDIM
    pick_head = (head_of[:, None] == jnp.arange(head_count)[None, :]).astype(jnp.bfloat16)
    log_rows = jnp.dot(pick_head, log_decay, preferred_element_type=jnp.float32)
    owners = lax.axis_size("seq")
    units = channels // UNIT
    capacity = units // owners + 1
    slot_count = capacity * owners
    width = capacity * UNIT

    def pack(values):
        padded = jnp.pad(values, ((0, slot_count * UNIT - channels), (0, 0)))
        return padded.reshape(owners, width, tokens_here)

    owned_x, owned_grad, owned_log = (
        lax.all_to_all(pack(x_rows), "seq", split_axis=0, concat_axis=2, tiled=True),
        lax.all_to_all(pack(y_grads), "seq", split_axis=0, concat_axis=2, tiled=True),
        lax.all_to_all(
            pack(log_rows.astype(jnp.bfloat16)), "seq", split_axis=0, concat_axis=2, tiled=True
        ),
    )
    b_all, c_all, start_all = (
        lax.all_gather(b_proj, "seq", axis=1, tiled=True),
        lax.all_gather(c_proj, "seq", axis=1, tiled=True),
        lax.all_gather(doc_start.astype(jnp.bfloat16), "seq", axis=0, tiled=True),
    )
    span = start_all.shape[0]
    marks = start_all.astype(jnp.int32) * (jnp.arange(span) > 0).astype(jnp.int32)
    owner_index = lax.axis_index("seq")

    def own(values):
        leading = values.shape[:-1]
        padded = jnp.pad(values, [(0, 0)] * len(leading) + [(0, slot_count * UNIT - channels)])
        return lax.dynamic_slice_in_dim(padded, owner_index * width, width, len(leading))

    x_own = owned_x.reshape(width, span)
    grad_own = owned_grad.reshape(width, span)
    log_own = owned_log.reshape(width, span).astype(jnp.float32)
    entry_own = own(entry_state)
    parts = prepare(x_own, grad_own, log_own, marks, b_all, c_all)
    edges = block_scans(parts)
    ssm_own, xgrad_own, b_part, c_part = finish(
        parts, edges, entry_own, jnp.zeros_like(entry_own), own(d_skip), x_own, grad_own
    )
    ssm_back, xgrad_back = (
        lax.all_to_all(
            ssm_own.reshape(1, width, span), "seq", split_axis=2, concat_axis=0, tiled=True
        ),
        lax.all_to_all(
            xgrad_own.reshape(1, width, span), "seq", split_axis=2, concat_axis=0, tiled=True
        ),
    )
    ssm_rows = ssm_back.reshape(slot_count * UNIT, tokens_here)[:channels]
    x_grad = xgrad_back.reshape(slot_count * UNIT, tokens_here)[:channels]
    state_size = b_part.shape[0]
    b_pieces, c_pieces = (
        lax.all_to_all(
            b_part.reshape(state_size, owners, tokens_here),
            "seq",
            split_axis=1,
            concat_axis=1,
            tiled=True,
        ),
        lax.all_to_all(
            c_part.reshape(state_size, owners, tokens_here),
            "seq",
            split_axis=1,
            concat_axis=1,
            tiled=True,
        ),
    )
    b_local = jnp.sum(b_pieces, axis=1)
    c_local = jnp.sum(c_pieces, axis=1)
    b_grad, c_grad = lax.psum((b_local, c_local), "tp")
    pre_grad = (x_grad.astype(jnp.float32) * silu_slope(pre_act)).astype(jnp.bfloat16)
    gate_grad = (mix_grad * ssm_rows.astype(jnp.float32) * silu_slope(gate_act)).astype(
        jnp.bfloat16
    )
    outer = (((0,), (0,)), ((), ()))
    from_pre = lax.dot_general(pre_grad, w_in, outer, preferred_element_type=jnp.float32)
    from_gate = lax.dot_general(gate_grad, w_gate, outer, preferred_element_type=jnp.float32)
    input_grad = lax.psum_scatter(
        from_pre + from_gate, "tp", scatter_dimension=0, tiled=True
    ).astype(jnp.bfloat16)
    return (input_grad, b_grad, c_grad)


def solution(mesh):
    in_specs = (
        P(("seq", "tp"), None),
        P(("seq", "tp"), None),
        P("tp", None),
        P("tp", None),
        P("tp", None),
        P(None, "seq"),
        P(None, "seq"),
        P(None, "seq"),
        P("tp"),
        P(None, "tp"),
        P("seq"),
    )
    out_specs = (P(("seq", "tp"), None), P(None, "seq"), P(None, "seq"))
    return jax.shard_map(shards, mesh=mesh, in_specs=in_specs, out_specs=out_specs, check_vma=False)
```

profile of v0, /device:TPU:1, one launch (start us, length us, event | category | flops | bytes accessed | tf_op | source)
XLA Modules:
  0.0 1350.9 jit_solution(8549044772882182733)
XLA Ops:
  9.0 21.0 %all-to-all-start = ((bf16[128,4,128]{2,1,0:T(4,128)(2,1)}), bf16[128,4,128]{2,1,0:T(4,128)(2,1)}, u32[]{:S(2)}, u32[]{:S(2)}) async-start(bf16[128,4,128]{2,1,0:T(4,128)(2,1)} %bitcast.15), calls=%async_computation | async-start | bytes 262144 | tf_op jit(solution)/shard_map/all_to_all | solution.py:187
  30.7 78.0 %all-gather = bf16[128,1,128]{2,1,0:T(2,128)(2,1)S(1)} all-gather(bf16[1,1,128]{2,1,0:T(2,128)(2,1)S(1)} %convert_bitcast_fusion.2), channel_id=1, replica_groups=mesh['seq'=128,'tp'=4] {'seq'}, dimensions={0}, use_global_device_ids=true | all-gather | bytes 33024 | tf_op jit(solution)/shard_map/all_gather | solution.py:194
  110.9 10.6 all_gather.15
  123.9 9.7 all_gather.19
  135.5 104.1 %all_gather.18 = bf16[16,16384]{1,0:T(8,128)(2,1)S(1)} all-gather(bf16[16,128]{1,0:T(8,128)(2,1)S(1)} %copy-done.44), channel_id=1, replica_groups=mesh['seq'=128,'tp'=4] {'seq'}, dimensions={1}, use_global_device_ids=true | all-gather | bytes 528384 | tf_op jit(solution)/shard_map/all_gather | solution.py:192
  239.7 99.9 %all_gather.17 = bf16[16,16384]{1,0:T(8,128)(2,1)S(1)} all-gather(bf16[16,128]{1,0:T(8,128)(2,1)S(1)} %copy-done.45), channel_id=1, replica_groups=mesh['seq'=128,'tp'=4] {'seq'}, dimensions={1}, use_global_device_ids=true | all-gather | bytes 528384 | tf_op jit(solution)/shard_map/all_gather | solution.py:193
  341.8 11.6 all-to-all-start.2
  406.3 16.6 %all-to-all-start.1 = ((bf16[128,4,128]{2,1,0:T(4,128)(2,1)}), bf16[128,4,128]{2,1,0:T(4,128)(2,1)}, u32[]{:S(2)}, u32[]{:S(2)}) async-start(bf16[128,4,128]{2,1,0:T(4,128)(2,1)} %bitcast.328), calls=%async_computation.1 | async-start | bytes 262144 | tf_op jit(solution)/shard_map/all_to_all | solution.py:185
  431.1 8.8 all-to-all-done.1
  443.3 2.5 multiply_multiply_fusion.1
  447.6 2.0 convolution_bitcast_fusion
  461.0 2.1 convolution_bitcast_fusion.1
  469.2 3.1 pad.216
  475.2 3.0 pad.217
  478.2 4.5 pad.218
  486.2 5.6 pad.219
  491.8 8.2 pad.220
  502.4 10.2 pad.221
  512.6 14.7 %pad.222 = f32[64,16,4]{1,2,0:T(4,128)} pad(f32[32,16,4]{1,2,0:T(4,128)} %add.402, f32[]{:T(128)} %constant.73.clone.1), padding=1_0_1x0_0_0x0_0_0 | pad | bytes 24580 | tf_op jit(solution)/shard_map/pad | solution.py:72
  530.9 28.6 %pad.307 = f32[127,16,4]{1,2,0:T(4,128)} pad(f32[64,16,4]{1,2,0:T(4,128)} %pad_maximum_fusion, f32[]{:T(128)} %constant.73.clone.1), padding=0_0_1x0_0_0x0_0_0 | pad | bytes 48900 | tf_op jit(solution)/shard_map/slice | solution.py:78
  559.4 28.4 %pad.389 = f32[128,16,4]{1,2,0:T(4,128)} pad(f32[64,16,4]{1,2,0:T(4,128)} %add.404, f32[]{:T(128)} %constant.73.clone.1), padding=1_0_1x0_0_0x0_0_0 | pad | bytes 49156
  595.4 3.2 pad.245
  601.4 3.0 pad.246
  604.3 4.5 pad.247
  612.4 5.6 pad.248
  618.0 8.2 pad.249
  628.6 10.2 pad.250
  638.8 14.7 %pad.251 = f32[64,16,4]{1,2,0:T(4,128)} pad(f32[32,16,4]{1,2,0:T(4,128)} %add.431, f32[]{:T(128)} %constant.73.clone.1), padding=1_0_1x0_0_0x0_0_0 | pad | bytes 24580 | tf_op jit(solution)/shard_map/pad | solution.py:73
  657.0 28.4 %pad.309 = f32[127,16,4]{1,2,0:T(4,128)} pad(f32[64,16,4]{1,2,0:T(4,128)} %pad_maximum_fusion.1, f32[]{:T(128)} %constant.73.clone.1), padding=0_0_1x0_0_0x0_0_0 | pad | bytes 48900 | tf_op jit(solution)/shard_map/slice | solution.py:82
  685.4 28.4 %pad.390 = f32[128,16,4]{1,2,0:T(4,128)} pad(f32[64,16,4]{1,2,0:T(4,128)} %add.433, f32[]{:T(128)} %constant.73.clone.1), padding=1_0_1x0_0_0x0_0_0 | pad | bytes 49156
  723.1 159.8 %while.16 = (s32[]{:T(128)}, f32[8,16,4,128]{3,2,1,0:T(4,128)}, f32[8,16,4,128]{3,2,1,0:T(4,128)}, f32[8,16,16,128]{3,2,1,0:T(8,128)}, f32[8,16,16,128]{3,2,1,0:...) while((s32[]{:T(128)}, f32[8,16,4,128]{3,2,1,0:T(4,128)}, ...), condition=%wide.region_3.4_spmd, body=%wide.region_2.3_spmd.sunk | while | flops 196837376 | bytes 9109941 | solution.py:133
  729.0 2.1 convolution_select_fusion.5
  731.1 2.4 fusion.164
  749.0 2.1 convolution_select_fusion.5
  751.1 2.4 fusion.164
  769.0 2.1 convolution_select_fusion.5
  771.1 2.4 fusion.164
  788.9 2.1 convolution_select_fusion.5
  791.0 2.4 fusion.164
  795.1 2.0 convolution_select_fusion.4
  808.9 2.1 convolution_select_fusion.5
  811.0 2.4 fusion.164
  828.8 2.1 convolution_select_fusion.5
  830.9 2.4 fusion.164
  848.8 2.1 convolution_select_fusion.5
  850.9 2.4 fusion.164
  868.7 2.1 convolution_select_fusion.5
  870.8 2.4 fusion.164
  886.3 12.9 copy.366
  899.8 91.3 %reduce.13 = bf16[16384,4]{1,0:T(8,128)(2,1)} reduce(bf16[16384,1,4]{2,1,0:T(2,128)(2,1)} %bitcast.304, bf16[]{:T(256)} %broadcast.279), dimensions={1}, to_apply=%bitcast.187.reduce_sub_computation | reduce | bytes 262146
  991.1 9.3 reshape.352
  1000.3 7.7 all-to-all-start.4
  1008.0 12.9 copy.360
  1021.0 90.9 %reduce.12 = bf16[16384,4]{1,0:T(8,128)(2,1)} reduce(bf16[16384,1,4]{2,1,0:T(2,128)(2,1)} %bitcast.305, bf16[]{:T(256)} %broadcast.279), dimensions={1}, to_apply=%bitcast.185.reduce_sub_computation | reduce | bytes 262146
  1111.8 8.7 reshape.350
  1120.6 33.4 %all_to_all.67 = bf16[128,2,256]{2,1,0:T(2,128)(2,1)} all-to-all(bf16[128,2,256]{2,1,0:T(2,128)(2,1)S(1)} %reshape.350), channel_id=1, replica_groups=mesh['seq'=128,'tp'=4] {'seq'}, dimensions={0} | all-to-all | bytes 262144 | tf_op jit(solution)/shard_map/all_to_all | solution.py:218
  1154.0 60.7 %all_to_all.68 = f32[16,128,128]{2,0,1:T(8,128)S(1)} all-to-all(f32[16,128,128]{2,0,1:T(8,128)S(1)} %bitcast.317), channel_id=1, replica_groups=mesh['seq'=128,'tp'=4] {'seq'}, dimensions={1} | all-to-all | bytes 2097152 | tf_op jit(solution)/shard_map/all_to_all | solution.py:233
  1214.7 8.7 all-to-all-start.5
  1223.5 19.4 %reshape.353 = bf16[16384,1,4]{2,1,0:T(2,128)(2,1)} reshape(bf16[128,2,256]{2,1,0:T(2,128)(2,1)} %copy-done.18) | data formatting | bytes 262144
  1242.8 16.4 %copy.367 = bf16[1,4,16384]{2,1,0:T(4,128)(2,1)} copy(bf16[1,4,16384]{1,0,2:T(2,128)(2,1)} %bitcast.306) | data formatting | bytes 262144 | tf_op jit(solution)/shard_map/all_to_all | solution.py:215
  1260.9 19.4 %reshape.351 = bf16[16384,1,4]{2,1,0:T(2,128)(2,1)} reshape(bf16[128,2,256]{2,1,0:T(2,128)(2,1)} %all_to_all.67) | data formatting | bytes 262144
  1280.2 16.4 %copy.361 = bf16[1,4,16384]{2,1,0:T(4,128)(2,1)} copy(bf16[1,4,16384]{1,0,2:T(2,128)(2,1)} %bitcast.307) | data formatting | bytes 262144 | tf_op jit(solution)/shard_map/all_to_all | solution.py:218
  1300.7 29.8 %reduce-scatter.2.cloned.1.call-done = f32[32,1600]{1,0:T(8,128)} async-done(((f32[128,1600]{1,0:T(8,128)}), f32[32,1600]{1,0:T(8,128)}) %reduce-scatter.2.cloned.1.call-update) | async-done | bytes 204816 | tf_op jit(solution)/shard_map/reduce_scatter | solution.py:251
  1332.4 11.4 all-reduce.65
  (530 shorter events, 268.7 us)
Async XLA Ops:
  7.2 114.9 %copy-start = (bf16[400,1600]{1,0:T(8,128)(2,1)S(1)}, bf16[400,1600]{1,0:T(8,128)(2,1)}, u32[]{:S(2)}) copy-start(bf16[400,1600]{1,0:T(8,128)(2,1)} %param.15) | copy-start | bytes 3840004
  7.2 102.1 %copy-start.31 = (f32[16,400]{1,0:T(8,128)S(1)}, f32[16,400]{1,0:T(8,128)}, u32[]{:S(2)}) copy-start(f32[16,400]{1,0:T(8,128)} %param.22) | copy-start | bytes 76804
  7.2 103.7 %copy-start.27 = (bf16[32,1600]{1,0:T(8,128)(2,1)S(1)}, bf16[32,1600]{1,0:T(8,128)(2,1)}, u32[]{:S(2)}) copy-start(bf16[32,1600]{1,0:T(8,128)(2,1)} %param.13) | copy-start | bytes 307204
  7.2 114.3 %copy-start.1 = (bf16[400,1600]{1,0:T(8,128)(2,1)S(1)}, bf16[400,1600]{1,0:T(8,128)(2,1)}, u32[]{:S(2)}) copy-start(bf16[400,1600]{1,0:T(8,128)(2,1)} %param.16) | copy-start | bytes 3840004
  9.0 332.8 %all-to-all-start = ((bf16[128,4,128]{2,1,0:T(4,128)(2,1)}), bf16[128,4,128]{2,1,0:T(4,128)(2,1)}, u32[]{:S(2)}, u32[]{:S(2)}) async-start(bf16[128,4,128]{2,1,0:T(4,128)(2,1)} %bitcast.15), calls=%async_computation | async-start | bytes 262144 | tf_op jit(solution)/shard_map/all_to_all | solution.py:187
  109.2 231.9 %copy-start.19 = (s32[128,128]{1,0:T(8,128)}, s32[128,128]{1,0:T(8,128)S(1)}, u32[]{:S(2)}) copy-start(s32[128,128]{1,0:T(8,128)S(1)} %copy.318) | copy-start | bytes 196612
  110.9 230.2 %copy-start.22 = (f32[128,128]{0,1:T(8,128)}, f32[128,128]{0,1:T(8,128)S(1)}, u32[]{:S(2)}) copy-start(f32[128,128]{0,1:T(8,128)S(1)} %get-tuple-element.226) | copy-start | bytes 196612
  122.0 11.6 copy-start.16
  122.0 1.9 copy-start.28
  122.0 11.6 copy-start.52
  133.6 1.9 copy-start.44
  134.8 104.8 %copy-start.45 = (bf16[16,128]{1,0:T(8,128)(2,1)S(1)}, bf16[16,128]{1,0:T(8,128)(2,1)}, u32[]{:S(2)}) copy-start(bf16[16,128]{1,0:T(8,128)(2,1)} %param.19) | copy-start | bytes 12292
  239.6 100.2 %copy-start.3 = (bf16[16,16384]{1,0:T(8,128)(2,1)}, bf16[16,16384]{1,0:T(8,128)(2,1)S(1)}, u32[]{:S(2)}) copy-start(bf16[16,16384]{1,0:T(8,128)(2,1)S(1)} %all_gather.18) | copy-start | bytes 1572868
  339.6 0.8 copy-start.4
  339.7 0.7 copy-start.50
  341.8 64.6 %all-to-all-start.2 = ((bf16[128,4,128]{2,1,0:T(4,128)(2,1)}), bf16[128,4,128]{2,1,0:T(4,128)(2,1)}, u32[]{:S(2)}, u32[]{:S(2)}) async-start(bf16[128,4,128]{2,1,0:T(4,128)(2,1)} %bitcast.329), calls=%async_computation.2 | async-start | bytes 262144 | tf_op jit(solution)/shard_map/all_to_all | solution.py:186
  356.2 0.7 copy-start.5
  387.9 55.4 %copy-start.23 = (f32[128,128]{0,1:T(8,128)S(1)}, f32[128,128]{0,1:T(8,128)}, u32[]{:S(2)}) copy-start(f32[128,128]{0,1:T(8,128)} %copy-done.22) | copy-start | bytes 196612
  406.3 33.6 %all-to-all-start.1 = ((bf16[128,4,128]{2,1,0:T(4,128)(2,1)}), bf16[128,4,128]{2,1,0:T(4,128)(2,1)}, u32[]{:S(2)}, u32[]{:S(2)}) async-start(bf16[128,4,128]{2,1,0:T(4,128)(2,1)} %bitcast.328), calls=%async_computation.1 | async-start | bytes 262144 | tf_op jit(solution)/shard_map/all_to_all | solution.py:185
  445.8 5.4 copy-start.40
  445.8 5.4 copy-start.41
  445.8 5.4 copy-start.42
  445.8 5.8 copy-start.39
  445.8 5.9 copy-start.38
  449.7 0.8 copy-start.9
  457.4 8.6 copy-start.33
  457.4 9.3 copy-start.35
  461.0 6.5 copy-start.47
  461.0 6.6 copy-start.49
  461.0 6.6 copy-start.51
  463.1 0.7 copy-start.8
  463.9 0.6 copy-start.15
  465.4 37.0 %slice-start.3 = ((f32[64,16,4]{1,2,0:T(4,128)}), f32[1,16,4]{1,2,0:T(4,128)S(1)}, s32[]{:S(2)}) async-start(f32[64,16,4]{1,2,0:T(4,128)} %copy-done.15), calls=%async_computation.12 | async-start | bytes 4096 | tf_op jit(solution)/shard_map/slice | solution.py:72
  466.1 0.6 copy-start.25
  472.4 57.8 %slice-start = ((f32[128,16,4]{1,2,0:T(4,128)}), f32[1,16,4]{1,2,0:T(4,128)S(1)}, s32[]{:S(2)}) async-start(f32[128,16,4]{1,2,0:T(4,128)} %copy-done.8), calls=%async_computation.9 | async-start | bytes 4096 | tf_op jit(solution)/shard_map/slice | solution.py:72
  512.6 77.0 %copy-start.30 = (f32[32,4]{1,0:T(8,128)S(1)}, f32[32,4]{1,0:T(8,128)}, u32[]{:S(2)}) copy-start(f32[32,4]{1,0:T(8,128)} %copy.342) | copy-start | bytes 1540
  527.3 63.0 %copy-start.32 = (f32[16,4]{1,0:T(8,128)S(1)}, f32[16,4]{1,0:T(8,128)}, u32[]{:S(2)}) copy-start(f32[16,4]{1,0:T(8,128)} %copy.344) | copy-start | bytes 772
  527.4 63.7 %copy-start.34 = (f32[8,4]{1,0:T(8,128)S(1)}, f32[8,4]{1,0:T(8,128)}, u32[]{:S(2)}) copy-start(f32[8,4]{1,0:T(8,128)} %copy.346) | copy-start | bytes 388
  527.4 64.3 %copy-start.43 = (f32[4,4]{1,0:T(4,128)S(1)}, f32[4,4]{1,0:T(4,128)}, u32[]{:S(2)}) copy-start(f32[4,4]{1,0:T(4,128)} %copy.348) | copy-start | bytes 196
  527.4 64.4 %copy-start.46 = (f32[2,4]{1,0:T(2,128)S(1)}, f32[2,4]{1,0:T(2,128)}, u32[]{:S(2)}) copy-start(f32[2,4]{1,0:T(2,128)} %copy.349) | copy-start | bytes 100
  529.0 70.9 %copy-start.36 = (f32[7,4]{1,0:T(8,128)S(1)}, f32[7,4]{1,0:T(8,128)}, u32[]{:S(2)}) copy-start(f32[7,4]{1,0:T(8,128)} %copy.345) | copy-start | bytes 340
  589.0 0.6 copy-start.14
  589.7 38.9 %slice-start.2 = ((f32[64,16,4]{1,2,0:T(4,128)}), f32[1,16,4]{1,2,0:T(4,128)S(1)}, s32[]{:S(2)}) async-start(f32[64,16,4]{1,2,0:T(4,128)} %copy-done.14), calls=%async_computation.11 | async-start | bytes 4096 | tf_op jit(solution)/shard_map/slice | solution.py:73
  590.4 0.6 copy-start.26
  598.5 57.8 %slice-start.1 = ((f32[128,16,4]{1,2,0:T(4,128)}), f32[1,16,4]{1,2,0:T(4,128)S(1)}, s32[]{:S(2)}) async-start(f32[128,16,4]{1,2,0:T(4,128)} %copy-done.9), calls=%async_computation.10 | async-start | bytes 4096 | tf_op jit(solution)/shard_map/slice | solution.py:73
  713.8 7.5 copy-start.37
  715.6 6.6 copy-start.20
  715.6 6.6 copy-start.29
  717.4 4.8 copy-start.7
  717.4 4.8 copy-start.21
  882.9 2.3 copy-start.6
  883.9 1.9 copy-start.10
  884.0 1.9 copy-start.11
  884.0 1.9 copy-start.48
  1000.3 120.3 %all-to-all-start.4 = ((bf16[128,2,256]{2,1,0:T(2,128)(2,1)}), bf16[128,2,256]{2,1,0:T(2,128)(2,1)S(1)}, u32[]{:S(2)}, u32[]{:S(2)}) async-start(bf16[128,2,256]{2,1,0:T(2,128)(2,1)} %reshape.352), calls=%async_computation.4 | async-start | bytes 262144 | tf_op jit(solution)/shard_map/all_to_all | solution.py:215
  1111.8 42.2 %copy-start.12 = (f32[8,16,16,128]{3,2,1,0:T(8,128)S(1)}, f32[8,16,16,128]{3,2,1,0:T(8,128)}, u32[]{:S(2)}) copy-start(f32[8,16,16,128]{3,2,1,0:T(8,128)} %get-tuple-element.86) | copy-start | bytes 3145732
  1120.6 33.4 %copy-start.18 = (bf16[128,2,256]{2,1,0:T(2,128)(2,1)}, bf16[128,2,256]{2,1,0:T(2,128)(2,1)S(1)}, u32[]{:S(2)}) copy-start(bf16[128,2,256]{2,1,0:T(2,128)(2,1)S(1)} %all-to-all-done.4) | copy-start | bytes 393220
  1214.7 117.6 %all-to-all-start.5 = ((f32[16,128,128]{2,0,1:T(8,128)}), f32[16,128,128]{2,0,1:T(8,128)S(1)}, u32[]{:S(2)}, u32[]{:S(2)}) async-start(f32[16,128,128]{2,0,1:T(8,128)} %bitcast.318), calls=%async_computation.6 | async-start | bytes 2097152 | tf_op jit(solution)/shard_map/all_to_all | solution.py:226
  1223.4 107.2 %reduce-scatter.2.cloned.1.call-start = ((), (), s32[]{:S(2)}) async-start(), calls=%async_computation.8 | async-start | bytes 1064960 | tf_op jit(solution)/shard_map/reduce_scatter | solution.py:251
  1297.6 1.6 copy-start.2
  1297.6 1.6 copy-start.13
  1297.7 1.6 copy-start.17
  1297.7 1.6 copy-start.24
Sparse Core Ops, SparseCore 0:
  1300.9 29.6 reduce-scatter.1
where the time goes:
time: 1380 us; the launch traced here: 1350 us
  local copies, waits for them, and re-layouts  432 us (31%)
  blocking collectives  408 us (30%)
  other arithmetic  248 us (18%)
  matrix products  144 us (10%)
  starting transfers between devices  65.7 us (5%)
  waiting for transfers between devices  38.6 us (3%)
  between operations  15.2 us (1%)
    unnamed x3, other arithmetic  183 us
    unnamed x116, local copies, waits for them, and re-layouts  120 us
    all_gather x1, blocking collectives, shards(): lax.all_gather(b_proj, 'seq', axis=1, tiled=True)  104 us
    all_gather x1, blocking collectives, shards(): lax.all_gather(c_proj, 'seq', axis=1, tiled=True)  99.9 us
    all_gather x1, blocking collectives, shards(): lax.all_gather(doc_start.astype(jnp.bfloat16), 'seq', axis=0, tiled=True)  78 us
    all_to_all x1, blocking collectives, shards(): lax.all_to_all(c_part.reshape(state_size, owners, tokens_here), 'seq', sp...  60.7 us
    pad x22, local copies, waits for them, and re-layouts, block_scans(): lax.associative_scan(combine_pairs, (factor, state_part))  54.8 us
    pad x22, local copies, waits for them, and re-layouts, block_scans(): lax.associative_scan(combine_pairs, (factor, grad_part), reverse=True)  54.8 us
  transfers between devices with their start and end apart: 6, of which 2 were waited for; matrix products, arithmetic and copies ran while one was open for 19% of the time, Pallas kernels for 0%

commit v1 on v0

v1 whole, which is shorter than its diff:
```python
import functools

import jax
import jax.numpy as jnp
from jax import lax
from jax.experimental import pallas as pl
from jax.experimental.pallas import tpu as pltpu
from jax.sharding import PartitionSpec as P

HDIM = 64
LANES = 128
MESH = pl.DeviceIdType.MESH
F32 = jnp.float32
BF16 = jnp.bfloat16
NN = (((1,), (0,)), ((), ()))
NT = (((1,), (1,)), ((), ()))
TN = (((0,), (0,)), ((), ()))
CHUNKS = ((0, 512), (512, 1024), (1024, 1600))


def dot(a, b, dims):
    return lax.dot_general(a, b, dims, preferred_element_type=F32)


def parts(value, count):
    high = value.astype(BF16)
    if count == 1:
        return (high,)
    return (high, (value - high.astype(F32)).astype(BF16))


def mm(a, b, dims):
    total = None
    for i, left in enumerate(a):
        for j, right in enumerate(b):
            if i + j < 2:
                term = dot(left, right, dims)
                total = term if total is None else total + term
    return total


def one_minus_exp(u):
    series = 1.0 - u / 6.0
    for k in (5.0, 4.0, 3.0, 2.0):
        series = 1.0 - u / k * series
    return jnp.where(u < 0.25, u * series, 1.0 - jnp.exp(-u))


def kernel(
    row_len,
    groups,
    ways,
    x_hbm,
    g_hbm,
    wi_hbm,
    wg_hbm,
    wo_hbm,
    b_ref,
    c_ref,
    log_ref,
    skip_ref,
    entry_ref,
    doc_ref,
    out_ref,
    bg_ref,
    cg_ref,
    xbuf,
    gbuf,
    wi,
    wg,
    wo,
    entry_t,
    f_send,
    f_recv,
    f_pre,
    fy_buf,
    p_send,
    p_recv,
    res,
    land,
    t_buf,
    wide,
    bc_buf,
    rs_send,
    rs_recv,
    lsem,
    gs,
    gr,
    fs,
    fr,
    ys,
    yr,
    ps,
    pr,
    ts,
    tr,
    ss,
    sr,
    bs,
    br,
    rs,
    rr,
):
    me = lax.axis_index("seq")
    tp = lax.axis_index("tp")
    group = lax.div(me, row_len)
    rank = lax.rem(me, row_len)
    unit = lax.div(rank, 2)
    way = lax.rem(rank, 2)
    block = x_hbm.shape[0]
    tokens = ways * block
    channels = wi_hbm.shape[0]
    heads = log_ref.shape[0]
    state = b_ref.shape[0]
    tiles = p_recv.shape[1]
    spans = [(k, k * LANES, min(channels, (k + 1) * LANES)) for k in range(tiles)]

    local = [
        pltpu.make_async_copy(wi_hbm, wi, lsem.at[0]),
        pltpu.make_async_copy(wg_hbm, wg, lsem.at[1]),
        pltpu.make_async_copy(wo_hbm, wo, lsem.at[2]),
        pltpu.make_async_copy(x_hbm, xbuf.at[tp], lsem.at[3]),
        pltpu.make_async_copy(g_hbm, gbuf.at[tp], lsem.at[4]),
    ]
    for copy in local:
        copy.start()

    def row_peer(i):
        return group * row_len + lax.rem(rank + i, row_len)

    def group_peer(k):
        return lax.rem(group + k, groups) * row_len + rank

    def way_peer(k):
        return lax.rem(tp + k, ways)

    barrier = pltpu.get_barrier_semaphore()

    def greet(i, carry):
        pl.semaphore_signal(barrier, inc=1, device_id=(row_peer(i), tp), device_id_type=MESH)
        return carry

    lax.fori_loop(1, row_len, greet, 0)
    for k in range(1, groups):
        pl.semaphore_signal(barrier, inc=1, device_id=(group_peer(k), tp), device_id_type=MESH)
    for k in range(1, ways):
        pl.semaphore_signal(barrier, inc=1, device_id=(me, way_peer(k)), device_id_type=MESH)
    pl.semaphore_wait(barrier, row_len + groups + ways - 3)

    gathers = []
    for a, (src, dst) in enumerate(((x_hbm, xbuf), (g_hbm, gbuf))):
        for k in range(1, ways):
            copy = pltpu.make_async_remote_copy(
                src_ref=src,
                dst_ref=dst.at[tp],
                send_sem=gs.at[a, k - 1],
                recv_sem=gr.at[a, k - 1],
                device_id=(me, way_peer(k)),
                device_id_type=MESH,
            )
            copy.start()
            gathers.append(copy)

    def to_row(src_at, dst, send_sem, recv_sem):
        def send(i, carry):
            pltpu.make_async_remote_copy(
                src_ref=src_at(lax.rem(rank + i, row_len)),
                dst_ref=dst,
                send_sem=send_sem,
                recv_sem=recv_sem,
                device_id=(row_peer(i), tp),
                device_id_type=MESH,
            ).start()
            return carry

        lax.fori_loop(1, row_len, send, 0)

    def to_groups(buf, send_sem, recv_sem):
        copies = []
        for k in range(1, groups):
            copy = pltpu.make_async_remote_copy(
                src_ref=buf.at[group],
                dst_ref=buf.at[group],
                send_sem=send_sem.at[k - 1],
                recv_sem=recv_sem.at[k - 1],
                device_id=(group_peer(k), tp),
                device_id_type=MESH,
            )
            copy.start()
            copies.append(copy)
        return copies

    def wait_row(sem):
        every = p_recv.at[pl.ds(0, row_len - 1)]
        pltpu.make_async_copy(every, every, sem).wait()

    head_row = lax.broadcasted_iota(jnp.int32, (heads, channels), 0)
    chan_row = lax.broadcasted_iota(jnp.int32, (heads, channels), 1) + tp * channels
    low = head_row * HDIM
    pick = jnp.where((chan_row >= low) & (chan_row < low + HDIM), 1.0, 0.0).astype(BF16)
    logs = dot(log_ref[...], pick, TN)
    row_at = lax.broadcasted_iota(jnp.int32, (tokens, tokens), 0)
    col_at = lax.broadcasted_iota(jnp.int32, (tokens, tokens), 1)
    tri = jnp.where(row_at >= col_at, 1.0, 0.0).astype(BF16)
    eye = jnp.where(row_at == col_at, 1.0, 0.0).astype(BF16)
    cumulative = dot(tri, logs.astype(BF16), NN)
    at = lax.broadcasted_iota(jnp.int32, (1, tokens), 1) + me
    marks = jnp.where(at > 0, doc_ref[...], 0).astype(F32)
    marks_wide = jnp.broadcast_to(marks, (channels, tokens)).astype(BF16)
    marks_sq = jnp.broadcast_to(marks, (tokens, tokens)).astype(BF16)
    counts = dot(tri, marks_wide, NT)
    mark_col = dot(eye, marks_wide, NT)
    counts_col = dot(tri, marks_sq, NT)
    counts_row = dot(marks_sq, tri, NT)
    last = counts[tokens - 1 : tokens, :]
    total = cumulative[tokens - 1 : tokens, :]
    factor = jnp.where(last == 0.0, jnp.exp(total), 0.0)

    f_send[...] = jnp.zeros_like(f_send)
    for k, lo, hi in spans:
        f_send[k : k + 1, 0 : hi - lo] = factor[:, lo:hi]
    f_recv[rank] = f_send[...]
    to_row(lambda peer: f_send, f_recv.at[rank], fs, fr)

    p_send[...] = jnp.zeros_like(p_send)
    entry_t[...] = jnp.zeros_like(entry_t)
    entry = entry_ref[...]
    for k, lo, hi in spans:
        entry_t[:, k, 0 : hi - lo] = entry[:, lo:hi]

    scales = jnp.where(mark_col == 1.0, 1.0, jnp.sqrt(one_minus_exp(-2.0 * logs)))
    centre = cumulative[tokens // 2 : tokens // 2 + 1, :]
    rising = jnp.exp(cumulative - centre)
    falling = jnp.exp(centre - cumulative)
    carry_in = jnp.where(counts == 0.0, jnp.exp(cumulative), 0.0)
    carry_out = jnp.where(counts == last, jnp.exp(total - cumulative), 0.0)
    causal = (row_at >= col_at) & (counts_col == counts_row)
    b_rows = b_ref[...]
    c_rows = c_ref[...]
    crossed = jnp.where(causal, dot(c_rows, b_rows, TN), 0.0)
    skip = skip_ref[...]

    wait_row(fr)

    def at_step(i, count):
        return jnp.where(way == 0, i, count - 1 - i)

    def decay_step(i, product):
        j = at_step(i, row_len)
        f_pre[j] = product
        return product * f_recv[j]

    fy_buf[group] = lax.fori_loop(0, row_len, decay_step, jnp.ones((tiles, LANES), F32))
    decay_copies = to_groups(fy_buf, ys, yr)

    for copy in gathers[: ways - 1]:
        copy.wait_recv()
    local[3].wait()
    local[0].wait()
    rows = xbuf[...].reshape(tokens, x_hbm.shape[1])
    pre_act = dot(rows, wi[...], NT)
    local[1].wait()
    gate_act = dot(rows, wg[...], NT)
    pre_sig = jax.nn.sigmoid(pre_act)
    gate_sig = jax.nn.sigmoid(gate_act)
    x_rows = (pre_act * pre_sig).astype(BF16).astype(F32)
    gate_silu = gate_act * gate_sig
    scaled = x_rows * scales
    scaled_out = parts(scaled * carry_out, 2)
    state_part = mm((b_rows,), scaled_out, NN)
    for k, lo, hi in spans:
        p_send[:, 0, k, 0 : hi - lo] = state_part[:, lo:hi]
    for copy in gathers[ways - 1 :]:
        copy.wait_recv()
    local[4].wait()
    local[2].wait()
    mix_grad = dot(gbuf[...].reshape(tokens, g_hbm.shape[1]), wo[...], NT)
    y_grads = (mix_grad * gate_silu).astype(BF16).astype(F32)
    grads_in = parts(y_grads * carry_in, 2)
    grad_part = mm((c_rows,), grads_in, NN)
    for k, lo, hi in spans:
        p_send[:, 1, k, 0 : hi - lo] = grad_part[:, lo:hi]

    p_recv[rank] = p_send[unit, way]
    to_row(lambda peer: p_send.at[lax.div(peer, 2), lax.rem(peer, 2)], p_recv.at[rank], ps, pr)

    upper = parts(y_grads * rising, 2)
    lower = parts(scaled * falling, 2)
    weight = parts(jnp.where(causal, mm(upper, lower, NT), 0.0), 2)
    crossed_parts = parts(crossed, 2)
    ssm_own = rising * mm(crossed_parts, lower, NN) + skip * x_rows
    x_own = falling * mm(crossed_parts, upper, TN)
    c_own = mm((b_rows,), weight, NT)
    b_own = mm((c_rows,), weight, NN)
    pre_slope = pre_sig * (1.0 + pre_act * (1.0 - pre_sig))
    gate_slope = mix_grad * (gate_sig * (1.0 + gate_act * (1.0 - gate_sig)))

    wait_row(pr)

    def scan_step(i, carried):
        j = at_step(i, row_len)
        res[j] = carried
        return f_recv[j] * carried + p_recv[j]

    t_buf[group] = lax.fori_loop(0, row_len, scan_step, jnp.zeros((tiles, LANES), F32))
    total_copies = to_groups(t_buf, ts, tr)
    for copy in decay_copies:
        copy.wait_recv()
    for copy in total_copies:
        copy.wait_recv()
    carried = jnp.where(way == 0, entry_t[unit], 0.0)
    ahead = at_step(group, groups)
    for i in range(groups):
        j = at_step(i, groups)
        carried = jnp.where(i < ahead, fy_buf[j] * carried + t_buf[j], carried)
    res[...] = res[...] + f_pre[...] * carried[None]
    land[unit, way] = res[rank]
    to_row(lambda peer: res.at[peer], land.at[unit, way], ss, sr)
    wait_row(sr)

    for k, lo, hi in spans:
        wide[0, :, lo : lo + LANES] = land[:, 0, k, :]
        wide[1, :, lo : lo + LANES] = land[:, 1, k, :]
    state_in = parts(wide[0, :, 0:channels], 2)
    grad_in = parts(wide[1, :, 0:channels], 2)
    bc_buf[tp, 0] = b_own + mm(grad_in, scaled_out, NT)
    bc_buf[tp, 1] = c_own + mm(state_in, grads_in, NT)
    bc_copies = []
    for k in range(1, ways):
        copy = pltpu.make_async_remote_copy(
            src_ref=bc_buf.at[tp],
            dst_ref=bc_buf.at[tp],
            send_sem=bs.at[k - 1],
            recv_sem=br.at[k - 1],
            device_id=(me, way_peer(k)),
            device_id_type=MESH,
        )
        copy.start()
        bc_copies.append(copy)
    ssm = (ssm_own + carry_in * mm((c_rows,), state_in, TN)).astype(BF16).astype(F32)
    x_part = x_own + carry_out * mm((b_rows,), grad_in, TN)
    x_grad = (x_part * scales + skip * y_grads).astype(BF16).astype(F32)
    pre_grad = (x_grad * pre_slope).astype(BF16)
    gate_grad = (ssm * gate_slope).astype(BF16)
    sums = []
    for i, (lo, hi) in enumerate(CHUNKS):
        part = dot(pre_grad, wi[:, lo:hi], NN) + dot(gate_grad, wg[:, lo:hi], NN)
        rs_send[:, :, lo:hi] = part.reshape(ways, block, hi - lo).astype(BF16)
        for k in range(1, ways):
            copy = pltpu.make_async_remote_copy(
                src_ref=rs_send.at[way_peer(k), :, lo:hi],
                dst_ref=rs_recv.at[k - 1, :, lo:hi],
                send_sem=rs.at[i, k - 1],
                recv_sem=rr.at[i, k - 1],
                device_id=(me, way_peer(k)),
                device_id_type=MESH,
            )
            copy.start()
            sums.append(copy)
    for copy in bc_copies:
        copy.wait_recv()
    both = bc_buf[0]
    for k in range(1, ways):
        both = both + bc_buf[k]
    bg_ref[...] = both[0]
    cg_ref[...] = both[1]
    for i, (lo, hi) in enumerate(CHUNKS):
        for copy in sums[i * (ways - 1) : (i + 1) * (ways - 1)]:
            copy.wait_recv()
        value = rs_send[tp, :, lo:hi].astype(F32)
        for k in range(ways - 1):
            value = value + rs_recv[k, :, lo:hi].astype(F32)
        out_ref[:, lo:hi] = value.astype(BF16)

    for copy in gathers + decay_copies + total_copies + bc_copies + sums:
        copy.wait_send()
    for sem in (fs, ps, ss):
        wait_row(sem)


def shards(
    layer_input,
    out_grad,
    w_in,
    w_gate,
    w_out,
    b_proj,
    c_proj,
    log_decay,
    d_skip,
    entry_state,
    doc_start,
):
    block, width = layer_input.shape
    channels = w_in.shape[0]
    state, tokens = b_proj.shape
    ways = lax.axis_size("tp")
    row_len = 2 * state
    groups = lax.axis_size("seq") // row_len
    tiles = -(-channels // LANES)
    anywhere = pl.BlockSpec(memory_space=pl.ANY)
    inside = pl.BlockSpec(memory_space=pltpu.VMEM)
    dma = pltpu.SemaphoreType.DMA
    return pl.pallas_call(
        functools.partial(kernel, row_len, groups, ways),
        out_shape=(
            jax.ShapeDtypeStruct((block, width), BF16),
            jax.ShapeDtypeStruct((state, tokens), F32),
            jax.ShapeDtypeStruct((state, tokens), F32),
        ),
        in_specs=[anywhere] * 5 + [inside] * 6,
        out_specs=(inside, inside, inside),
        scratch_shapes=[
            pltpu.VMEM((ways, block, width), BF16),
            pltpu.VMEM((ways, block, width), BF16),
            pltpu.VMEM((channels, width), BF16),
            pltpu.VMEM((channels, width), BF16),
            pltpu.VMEM((channels, width), BF16),
            pltpu.VMEM((state, tiles, LANES), F32),
            pltpu.VMEM((tiles, LANES), F32),
            pltpu.VMEM((row_len, tiles, LANES), F32),
            pltpu.VMEM((row_len, tiles, LANES), F32),
            pltpu.VMEM((groups, tiles, LANES), F32),
            pltpu.VMEM((state, 2, tiles, LANES), F32),
            pltpu.VMEM((row_len, tiles, LANES), F32),
            pltpu.VMEM((row_len, tiles, LANES), F32),
            pltpu.VMEM((state, 2, tiles, LANES), F32),
            pltpu.VMEM((groups, tiles, LANES), F32),
            pltpu.VMEM((2, state, tiles * LANES), F32),
            pltpu.VMEM((ways, 2, state, tokens), F32),
            pltpu.VMEM((ways, block, width), BF16),
            pltpu.VMEM((ways - 1, block, width), BF16),
            dma((5,)),
            dma((2, ways - 1)),
            dma((2, ways - 1)),
            dma,
            dma,
            dma((groups - 1,)),
            dma((groups - 1,)),
            dma,
            dma,
            dma((groups - 1,)),
            dma((groups - 1,)),
            dma,
            dma,
            dma((ways - 1,)),
            dma((ways - 1,)),
            dma((len(CHUNKS), ways - 1)),
            dma((len(CHUNKS), ways - 1)),
        ],
        compiler_params=pltpu.CompilerParams(
            collective_id=0, has_side_effects=True, vmem_limit_bytes=32 * 1024 * 1024
        ),
        name="gated_recurrence_backward",
    )(
        layer_input,
        out_grad,
        w_in,
        w_gate,
        w_out,
        b_proj,
        c_proj,
        log_decay,
        d_skip.reshape(1, channels),
        entry_state,
        doc_start.reshape(1, tokens),
    )


def solution(mesh):
    in_specs = (
        P(("seq", "tp"), None),
        P(("seq", "tp"), None),
        P("tp", None),
        P("tp", None),
        P("tp", None),
        P(None, "seq"),
        P(None, "seq"),
        P(None, "seq"),
        P("tp"),
        P(None, "tp"),
        P("seq"),
    )
    out_specs = (P(("seq", "tp"), None), P(None, "seq"), P(None, "seq"))
    return jax.shard_map(shards, mesh=mesh, in_specs=in_specs, out_specs=out_specs, check_vma=False)
```

time: 1380 us -> 73 us (0.05); the launches traced: 1350 us -> 72.5 us
  local copies, waits for them, and re-layouts: 432 us -> 11.8 us
  blocking collectives: 408 us -> 0 us
  other arithmetic: 248 us -> 0 us
  matrix products: 144 us -> 0 us
  starting transfers between devices: 65.7 us -> 0 us
  Pallas kernels: 0 us -> 60.1 us
  waiting for transfers between devices: 38.6 us -> 0 us
  between operations: 15.2 us -> 0.66 us
    all_gather x5 -> x0, blocking collectives: 302 us -> none  [the longest x1 104 us: shards(): lax.all_gather(b_proj, 'seq', axis=1, tiled=True)]
    unnamed x3 -> x0, other arithmetic: 183 us -> none
    dot_general x88 -> x0, matrix products: 144 us -> none  [the longest x8 19.2 us: block_pass(): jnp.dot(b_blk, weight.T, precision=FULL_PRECISION)]
    pad x47 -> x0, local copies, waits for them, and re-layouts: 112 us -> none  [the longest x22 54.8 us: block_scans(): lax.associative_scan(combine_pairs, (factor, state_part))]
    unnamed x116 -> x25, local copies, waits for them, and re-layouts: 120 us -> 11.8 us
    all_to_all x2 -> x0, blocking collectives: 94.1 us -> none  [the longest x1 60.7 us: shards(): lax.all_to_all(c_part.reshape(state_size, owners, tokens_here), 'seq', sp...]
    slice x96 -> x0, local copies, waits for them, and re-layouts: 90.9 us -> none  [the longest x2 30.1 us: block_scans(): rev_grad[1:]]
    all_to_all x5 -> x0, starting transfers between devices: 65.7 us -> none  [the longest x1 21 us: shards(): lax.all_to_all(pack(log_rows.astype(jnp.bfloat16)), 'seq', split_axis=0,...]
  transfers between devices with their start and end apart: 6 -> 0, of which waited for: 2 -> 0; matrix products, arithmetic and copies ran while one was open for 19% -> 0% of each run, Pallas kernels for 0% -> 0%
where the time goes in v1:
time: 73 us; the launch traced here: 72.5 us
  Pallas kernels  60.1 us (82%)
  local copies, waits for them, and re-layouts  11.8 us (16%)
    pallas_call x1, Pallas kernels, shards(): pl.pallas_call(functools.partial(kernel, row_len, groups, ways), out_shap...  60.1 us
    unnamed x25, local copies, waits for them, and re-layouts  11.8 us

profile of v1, /device:TPU:1, one launch (start us, length us, event | category | flops | bytes accessed | tf_op | source)
XLA Modules:
  0.0 72.5 jit_solution(13657310837381617353)
XLA Ops:
  0.6 0.0 copy-start
  0.6 1.3 %copy-done = bf16[400,1600]{1,0:T(8,128)(2,1)S(1)} copy-done((bf16[400,1600]{1,0:T(8,128)(2,1)S(1)}, bf16[400,1600]{1,0:T(8,128)(2,1)}, u32[]{:S(2)}) %copy-start) | copy-done | bytes 1280024
  2.0 0.0 copy-start.1
  2.0 1.3 %copy-done.1 = bf16[400,1600]{1,0:T(8,128)(2,1)S(1)} copy-done((bf16[400,1600]{1,0:T(8,128)(2,1)S(1)}, bf16[400,1600]{1,0:T(8,128)(2,1)}, u32[]{:S(2)}) %copy-start.1) | copy-done | bytes 1280024
  3.3 0.0 copy-start.2
  3.3 1.3 %copy-done.2 = bf16[400,1600]{1,0:T(8,128)(2,1)S(1)} copy-done((bf16[400,1600]{1,0:T(8,128)(2,1)S(1)}, bf16[400,1600]{1,0:T(8,128)(2,1)}, u32[]{:S(2)}) %copy-start.2) | copy-done | bytes 1280024
  4.6 0.0 copy-start.3
  4.6 0.9 %copy-done.3 = bf16[32,1600]{1,0:T(8,128)(2,1)S(1)} copy-done((bf16[32,1600]{1,0:T(8,128)(2,1)S(1)}, bf16[32,1600]{1,0:T(8,128)(2,1)}, u32[]{:S(2)}) %copy-start.3) | copy-done | bytes 102424
  5.5 0.0 copy-start.4
  5.5 0.9 %copy-done.4 = bf16[32,1600]{1,0:T(8,128)(2,1)S(1)} copy-done((bf16[32,1600]{1,0:T(8,128)(2,1)S(1)}, bf16[32,1600]{1,0:T(8,128)(2,1)}, u32[]{:S(2)}) %copy-start.4) | copy-done | bytes 102424
  6.4 0.0 copy-start.5
  6.4 0.8 %copy-done.5 = f32[16,400]{1,0:T(8,128)S(1)} copy-done((f32[16,400]{1,0:T(8,128)S(1)}, f32[16,400]{1,0:T(8,128)}, u32[]{:S(2)}) %copy-start.5) | copy-done | bytes 25624
  7.2 0.0 copy-start.6
  7.2 0.7 copy-done.6
  7.9 0.0 copy-start.7
  7.9 0.7 copy-done.7
  8.5 0.0 copy-start.8
  8.5 0.7 copy-done.8
  9.2 0.0 copy-start.9
  9.2 0.7 copy-done.9
  9.9 0.0 copy-start.10
  9.9 0.7 copy-done.10
  10.6 60.1 %gated_recurrence_backward.1 = (bf16[32,1600]{1,0:T(8,128)(2,1)S(1)}, f32[16,128]{1,0:T(8,128)S(1)}, f32[16,128]{1,0:T(8,128)S(1)}) custom-call(bf16[32,1600]{1,0:T(8,128)(2,1)S(1)} %copy-done.3, bf16[32,1600]{1,0:T(8,128)(2,1)S(1)} %copy-done.4, bf16[400,1600]{1,0:T(8,128)(2,1)S(1)} %copy-done, bf16[400,1600]{1,0:T(8,128)(2,1)S(1)} %copy-done.1, ...), custom_call_target="tpu_custom_call" | custom-call | tf_op jit(solution)/shard_map/gated_recurrence_backward/pallas_call | solution.py:404
  70.7 0.6 copy.17
  71.3 0.6 copy.18
  71.9 0.6 copy.19
Async XLA Ops:
  0.6 1.3 %copy-start = (bf16[400,1600]{1,0:T(8,128)(2,1)S(1)}, bf16[400,1600]{1,0:T(8,128)(2,1)}, u32[]{:S(2)}) copy-start(bf16[400,1600]{1,0:T(8,128)(2,1)} %wi_hbm.1) | copy-start | bytes 3840004
  2.0 1.3 %copy-start.1 = (bf16[400,1600]{1,0:T(8,128)(2,1)S(1)}, bf16[400,1600]{1,0:T(8,128)(2,1)}, u32[]{:S(2)}) copy-start(bf16[400,1600]{1,0:T(8,128)(2,1)} %wg_hbm.1) | copy-start | bytes 3840004
  3.3 1.3 %copy-start.2 = (bf16[400,1600]{1,0:T(8,128)(2,1)S(1)}, bf16[400,1600]{1,0:T(8,128)(2,1)}, u32[]{:S(2)}) copy-start(bf16[400,1600]{1,0:T(8,128)(2,1)} %wo_hbm.1) | copy-start | bytes 3840004
  4.6 0.9 %copy-start.3 = (bf16[32,1600]{1,0:T(8,128)(2,1)S(1)}, bf16[32,1600]{1,0:T(8,128)(2,1)}, u32[]{:S(2)}) copy-start(bf16[32,1600]{1,0:T(8,128)(2,1)} %x_hbm.1) | copy-start | bytes 307204
  5.5 0.9 %copy-start.4 = (bf16[32,1600]{1,0:T(8,128)(2,1)S(1)}, bf16[32,1600]{1,0:T(8,128)(2,1)}, u32[]{:S(2)}) copy-start(bf16[32,1600]{1,0:T(8,128)(2,1)} %g_hbm.1) | copy-start | bytes 307204
  6.4 0.8 %copy-start.5 = (f32[16,400]{1,0:T(8,128)S(1)}, f32[16,400]{1,0:T(8,128)}, u32[]{:S(2)}) copy-start(f32[16,400]{1,0:T(8,128)} %entry_ref.1) | copy-start | bytes 76804
  7.2 0.7 copy-start.6
  7.9 0.7 copy-start.7
  8.5 0.7 copy-start.8
  9.2 0.7 copy-start.9
  9.9 0.7 copy-start.10

commit v2 on v1

v2 whole, which is shorter than its diff:
```python
import functools

import jax
import jax.numpy as jnp
from jax import lax
from jax.experimental import pallas as pl
from jax.experimental.pallas import tpu as pltpu
from jax.sharding import PartitionSpec as P

HDIM = 64
LANES = 128
SETS_Z = 4
MESH = pl.DeviceIdType.MESH
F32 = jnp.float32
BF16 = jnp.bfloat16
NN = (((1,), (0,)), ((), ()))
NT = (((1,), (1,)), ((), ()))
TN = (((0,), (0,)), ((), ()))
CHUNKS = ((0, 768), (768, 1600))


def dot(a, b, dims):
    return lax.dot_general(a, b, dims, preferred_element_type=F32)


def parts(value, count):
    high = value.astype(BF16)
    if count == 1:
        return (high,)
    return (high, (value - high.astype(F32)).astype(BF16))


def mm(a, b, dims):
    total = None
    for i, left in enumerate(a):
        for j, right in enumerate(b):
            if i + j < 2:
                term = dot(left, right, dims)
                total = term if total is None else total + term
    return total


def one_minus_exp(u):
    series = 1.0 - u / 6.0
    for k in (5.0, 4.0, 3.0, 2.0):
        series = 1.0 - u / k * series
    return jnp.where(u < 0.25, u * series, 1.0 - jnp.exp(-u))


def kernel(
    row_len,
    groups,
    sets_z,
    ways,
    x_hbm,
    g_hbm,
    wi_hbm,
    wg_hbm,
    wo_hbm,
    b_hbm,
    c_hbm,
    log_hbm,
    skip_hbm,
    entry_hbm,
    doc_hbm,
    out_hbm,
    bg_hbm,
    cg_hbm,
    xbuf,
    gbuf,
    wi,
    wg,
    wo,
    b_ref,
    c_ref,
    log_ref,
    skip_ref,
    entry_ref,
    doc_ref,
    entry_t,
    f_send,
    f_recv,
    f_pre,
    fy_buf,
    p_send,
    p_recv,
    res,
    land,
    t_buf,
    wide,
    bc_buf,
    rs_send,
    rs_recv,
    out_ref,
    bg_ref,
    cg_ref,
    osem,
    heard,
    lsem,
    gs,
    gr,
    fs,
    fr,
    ys,
    yr,
    ps,
    pr,
    ts,
    tr,
    ss,
    sr,
    bs,
    br,
    rs,
    rr,
):
    me = lax.axis_index("seq")
    tp = lax.axis_index("tp")
    group = lax.div(me, row_len)
    rank = lax.rem(me, row_len)
    way = lax.rem(rank, 2)
    share = 2 * b_hbm.shape[0] // row_len
    block = x_hbm.shape[0]
    tokens = ways * block
    channels = wi_hbm.shape[0]
    heads = log_ref.shape[0]
    state = b_ref.shape[0]
    tiles = p_recv.shape[1] // share
    spans = [(k, k * LANES, min(channels, (k + 1) * LANES)) for k in range(tiles)]

    small = [
        pltpu.make_async_copy(src, dst, lsem.at[5 + i])
        for i, (src, dst) in enumerate(
            (
                (log_hbm, log_ref),
                (doc_hbm, doc_ref),
                (b_hbm, b_ref),
                (c_hbm, c_ref),
                (skip_hbm, skip_ref),
                (entry_hbm, entry_ref),
            )
        )
    ]
    local = [
        pltpu.make_async_copy(x_hbm, xbuf.at[tp], lsem.at[3]),
        pltpu.make_async_copy(g_hbm, gbuf.at[tp], lsem.at[4]),
        pltpu.make_async_copy(wi_hbm, wi, lsem.at[0]),
        pltpu.make_async_copy(wg_hbm, wg, lsem.at[1]),
        pltpu.make_async_copy(wo_hbm, wo, lsem.at[2]),
    ]
    for copy in local[:2] + small + local[2:]:
        copy.start()

    def row_peer(i):
        return group * row_len + lax.rem(rank + i, row_len)

    def way_peer(k):
        return lax.rem(tp + k, ways)

    line, spot = lax.div(group, sets_z), lax.rem(group, sets_z)
    lines = groups // sets_z
    last_line, last_spot = lines - 1 - line, sets_z - 1 - spot

    def by_way(forward_value, backward_value):
        return forward_value * (1 - way) + backward_value * way

    def each_set(act):
        def step(i, carry):
            other_spot, other_line = lax.div(i, lines), lax.rem(i, lines)
            other = other_line * sets_z + other_spot
            gap = (other - group) * (1 - 2 * way)
            act(other, gap, other_spot)
            return carry

        lax.fori_loop(0, groups, step, 0)

    def device_of(other):
        return (other * row_len + rank, tp)

    barrier = pltpu.get_barrier_semaphore()

    def greet(i, carry):
        pl.semaphore_signal(barrier, inc=1, device_id=(row_peer(i), tp), device_id_type=MESH)
        return carry

    def greet_set(other, gap, other_spot):
        @pl.when(((gap < 0) & (spot <= other_spot)) | ((gap > 0) & (spot < other_spot)))
        def _():
            pl.semaphore_signal(barrier, inc=1, device_id=device_of(other), device_id_type=MESH)

    def answer_set(other, gap, other_spot):
        @pl.when((gap < 0) & (spot > other_spot))
        def _():
            pl.semaphore_signal(heard, inc=1, device_id=device_of(other), device_id_type=MESH)

    for k in range(1, ways):
        pl.semaphore_signal(barrier, inc=1, device_id=(me, way_peer(k)), device_id_type=MESH)
    lax.fori_loop(1, row_len, greet, 0)
    each_set(greet_set)
    before = by_way(
        last_line * (spot + 1) + (line + 1) * spot,
        line * (spot + 1) + spot + last_line * spot,
    )
    after = by_way((last_line + 1) * last_spot, line * last_spot)
    pl.semaphore_wait(barrier, row_len + ways - 2 + before)

    half = block // 2
    right, left = way_peer(1), way_peer(ways - 1)
    gathers = []

    def pass_on(array, slot, part, to, landing):
        buf = (xbuf, gbuf)[array]
        where = buf.at[slot, pl.ds(part * half, half)]
        copy = pltpu.make_async_remote_copy(
            src_ref=where,
            dst_ref=where,
            send_sem=gs.at[array, landing],
            recv_sem=gr.at[array, landing],
            device_id=(me, to),
            device_id_type=MESH,
        )
        copy.start()
        gathers.append(copy)

    def landed(array, slot, part, landing):
        where = (xbuf, gbuf)[array].at[slot, pl.ds(part * half, half)]
        pltpu.make_async_copy(where, where, gr.at[array, landing]).wait()

    def forward(array):
        landed(array, left, 0, 0)
        pass_on(array, left, 0, right, 4)
        landed(array, right, 1, 3)
        pass_on(array, right, 1, left, 5)

    def gathered(array):
        landed(array, left, 1, 1)
        landed(array, right, 0, 2)
        landed(array, way_peer(2), 0, 4)
        landed(array, way_peer(2), 1, 5)

    for array in range(2):
        local[array].wait()
        pass_on(array, tp, 0, right, 0)
        pass_on(array, tp, 1, left, 3)
        pass_on(array, tp, 1, right, 1)
        pass_on(array, tp, 0, left, 2)
    each_set(answer_set)

    def to_row(src_at, dst, send_sem, recv_sem):
        def send(i, carry):
            pltpu.make_async_remote_copy(
                src_ref=src_at(lax.rem(rank + i, row_len)),
                dst_ref=dst,
                send_sem=send_sem,
                recv_sem=recv_sem,
                device_id=(row_peer(i), tp),
                device_id_type=MESH,
            ).start()
            return carry

        lax.fori_loop(1, row_len, send, 0)

    def set_copy(buf, other, source, send_sem, recv_sem):
        return pltpu.make_async_remote_copy(
            src_ref=buf.at[source],
            dst_ref=buf.at[source],
            send_sem=send_sem.at[other],
            recv_sem=recv_sem.at[source],
            device_id=device_of(other),
            device_id_type=MESH,
        )

    def to_sets(buf, send_sem, recv_sem):
        def send(other, gap, other_spot):
            @pl.when(gap > 0)
            def _():
                set_copy(buf, other, group, send_sem, recv_sem).start()

        each_set(send)

    def wait_sets(buf, send_sem, recv_sem, sent):
        def wait(other, gap, other_spot):
            if sent:

                @pl.when(gap > 0)
                def _():
                    set_copy(buf, other, group, send_sem, recv_sem).wait_send()

            else:

                @pl.when(gap < 0)
                def _():
                    set_copy(buf, other, other, send_sem, recv_sem).wait_recv()

        each_set(wait)

    def wait_row(sem):
        every = p_recv.at[pl.ds(0, row_len - 1)]
        pltpu.make_async_copy(every, every, sem).wait()

    for copy in small:
        copy.wait()
    head_row = lax.broadcasted_iota(jnp.int32, (heads, channels), 0)
    chan_row = lax.broadcasted_iota(jnp.int32, (heads, channels), 1) + tp * channels
    low = head_row * HDIM
    pick = jnp.where((chan_row >= low) & (chan_row < low + HDIM), 1.0, 0.0).astype(BF16)
    logs = dot(log_ref[...], pick, TN)
    row_at = lax.broadcasted_iota(jnp.int32, (tokens, tokens), 0)
    col_at = lax.broadcasted_iota(jnp.int32, (tokens, tokens), 1)
    tri = jnp.where(row_at >= col_at, 1.0, 0.0).astype(BF16)
    eye = jnp.where(row_at == col_at, 1.0, 0.0).astype(BF16)
    cumulative = dot(tri, logs.astype(BF16), NN)
    at = lax.broadcasted_iota(jnp.int32, (1, tokens), 1) + me
    marks = jnp.where(at > 0, doc_ref[...], 0).astype(F32)
    marks_wide = jnp.broadcast_to(marks, (channels, tokens)).astype(BF16)
    marks_sq = jnp.broadcast_to(marks, (tokens, tokens)).astype(BF16)
    counts = dot(tri, marks_wide, NT)
    mark_col = dot(eye, marks_wide, NT)
    counts_col = dot(tri, marks_sq, NT)
    counts_row = dot(marks_sq, tri, NT)
    last = counts[tokens - 1 : tokens, :]
    total = cumulative[tokens - 1 : tokens, :]
    factor = jnp.where(last == 0.0, jnp.exp(total), 0.0)

    f_send[...] = jnp.zeros_like(f_send)
    for k, lo, hi in spans:
        f_send[share * k : share * (k + 1), 0 : hi - lo] = jnp.broadcast_to(
            factor[:, lo:hi], (share, hi - lo)
        )
    f_recv[rank] = f_send[...]
    to_row(lambda peer: f_send, f_recv.at[rank], fs, fr)
    forward(0)

    p_send[...] = jnp.zeros_like(p_send)
    entry_t[...] = jnp.zeros_like(entry_t)

    def lay_out(rows, put):
        for q in range(state // share):
            for k, lo, hi in spans:
                put(q, slice(share * k, share * (k + 1)), slice(0, hi - lo), rows[share * q : share * (q + 1), lo:hi])

    def put_entry(q, rows, lanes, value):
        entry_t[q, rows, lanes] = value

    def put_state(q, rows, lanes, value):
        p_send[2 * q, rows, lanes] = value

    def put_grad(q, rows, lanes, value):
        p_send[2 * q + 1, rows, lanes] = value

    lay_out(entry_ref[...], put_entry)

    scales = jnp.where(mark_col == 1.0, 1.0, jnp.sqrt(one_minus_exp(-2.0 * logs)))
    centre = cumulative[tokens // 2 : tokens // 2 + 1, :]
    rising = jnp.exp(cumulative - centre)
    falling = jnp.exp(centre - cumulative)
    carry_in = jnp.where(counts == 0.0, jnp.exp(cumulative), 0.0)
    carry_out = jnp.where(counts == last, jnp.exp(total - cumulative), 0.0)
    causal = (row_at >= col_at) & (counts_col == counts_row)
    b_rows = b_ref[...]
    c_rows = c_ref[...]
    crossed = jnp.where(causal, dot(c_rows, b_rows, TN), 0.0)
    skip = skip_ref[...]

    forward(1)

    wait_row(fr)

    def at_step(i, count):
        return jnp.where(way == 0, i, count - 1 - i)

    def decay_step(i, product):
        j = at_step(i, row_len)
        f_pre[j] = product
        return product * f_recv[j]

    fy_buf[group] = lax.fori_loop(0, row_len, decay_step, jnp.ones(f_send.shape, F32))

    @pl.when(after > 0)
    def _():
        pl.semaphore_wait(heard, after)

    to_sets(fy_buf, ys, yr)

    gathered(0)
    local[2].wait()
    rows = xbuf[...].reshape(tokens, x_hbm.shape[1])
    pre_act = dot(rows, wi[...], NT)
    local[3].wait()
    gate_act = dot(rows, wg[...], NT)
    pre_sig = jax.nn.sigmoid(pre_act)
    gate_sig = jax.nn.sigmoid(gate_act)
    x_rows = (pre_act * pre_sig).astype(BF16).astype(F32)
    gate_silu = gate_act * gate_sig
    scaled = x_rows * scales
    scaled_out = parts(scaled * carry_out, 2)
    state_part = mm((b_rows,), scaled_out, NN)
    lay_out(state_part, put_state)
    gathered(1)
    local[4].wait()
    mix_grad = dot(gbuf[...].reshape(tokens, g_hbm.shape[1]), wo[...], NT)
    y_grads = (mix_grad * gate_silu).astype(BF16).astype(F32)
    grads_in = parts(y_grads * carry_in, 2)
    grad_part = mm((c_rows,), grads_in, NN)
    lay_out(grad_part, put_grad)

    p_recv[rank] = p_send[rank]
    to_row(lambda peer: p_send.at[peer], p_recv.at[rank], ps, pr)

    upper = parts(y_grads * rising, 2)
    lower = parts(scaled * falling, 2)
    weight = parts(jnp.where(causal, mm(upper, lower, NT), 0.0), 2)
    crossed_parts = parts(crossed, 2)
    ssm_own = rising * mm(crossed_parts, lower, NN) + skip * x_rows
    x_own = falling * mm(crossed_parts, upper, TN)
    c_own = mm((b_rows,), weight, NT)
    b_own = mm((c_rows,), weight, NN)
    pre_slope = pre_sig * (1.0 + pre_act * (1.0 - pre_sig))
    gate_slope = mix_grad * (gate_sig * (1.0 + gate_act * (1.0 - gate_sig)))

    wait_row(pr)

    def scan_step(i, carried):
        j = at_step(i, row_len)
        res[j] = carried
        return f_recv[j] * carried + p_recv[j]

    t_buf[group] = lax.fori_loop(0, row_len, scan_step, jnp.zeros(f_send.shape, F32))
    to_sets(t_buf, ts, tr)
    wait_sets(fy_buf, ys, yr, False)
    wait_sets(t_buf, ts, tr, False)
    carried = jnp.where(way == 0, entry_t[lax.div(rank, 2)], 0.0)
    ahead = at_step(group, groups)
    for i in range(groups):
        j = at_step(i, groups)
        carried = jnp.where(i < ahead, fy_buf[j] * carried + t_buf[j], carried)
    res[...] = res[...] + f_pre[...] * carried[None]
    land[rank] = res[rank]
    to_row(lambda peer: res.at[peer], land.at[rank], ss, sr)
    wait_row(sr)

    for q in range(state // share):
        for k, lo, hi in spans:
            for side in range(2):
                wide[side, share * q : share * (q + 1), lo : lo + LANES] = land[
                    2 * q + side, share * k : share * (k + 1), :
                ]
    state_in = parts(wide[0, :, 0:channels], 2)
    grad_in = parts(wide[1, :, 0:channels], 2)
    ssm = (ssm_own + carry_in * mm((c_rows,), state_in, TN)).astype(BF16).astype(F32)
    x_part = x_own + carry_out * mm((b_rows,), grad_in, TN)
    x_grad = (x_part * scales + skip * y_grads).astype(BF16).astype(F32)
    pre_grad = (x_grad * pre_slope).astype(BF16)
    gate_grad = (ssm * gate_slope).astype(BF16)
    bc_buf[tp, 0] = b_own + mm(grad_in, scaled_out, NT)
    bc_buf[tp, 1] = c_own + mm(state_in, grads_in, NT)
    bc_copies = []
    for k in range(1, ways):
        copy = pltpu.make_async_remote_copy(
            src_ref=bc_buf.at[tp],
            dst_ref=bc_buf.at[tp],
            send_sem=bs.at[k - 1],
            recv_sem=br.at[k - 1],
            device_id=(me, way_peer(k)),
            device_id_type=MESH,
        )
        copy.start()
        bc_copies.append(copy)
    order = (
        jnp.where(tp == 0, 3, jnp.where(tp == ways - 1, 1, 2)),
        jnp.where((tp == 0) | (tp == ways - 1), 2, 1),
        jnp.where(tp == 0, 1, 3),
    )
    sums = []
    for i, (lo, hi) in enumerate(CHUNKS):
        part = dot(pre_grad, wi[:, lo:hi], NN) + dot(gate_grad, wg[:, lo:hi], NN)
        rs_send[:, :, lo:hi] = part.reshape(ways, block, hi - lo).astype(BF16)
        for k in order:
            copy = pltpu.make_async_remote_copy(
                src_ref=rs_send.at[way_peer(k), :, lo:hi],
                dst_ref=rs_recv.at[k - 1, :, lo:hi],
                send_sem=rs.at[i, k - 1],
                recv_sem=rr.at[i, k - 1],
                device_id=(me, way_peer(k)),
                device_id_type=MESH,
            )
            copy.start()
            sums.append(copy)
    for copy in bc_copies:
        copy.wait_recv()
    both = bc_buf[0]
    for k in range(1, ways):
        both = both + bc_buf[k]
    bg_ref[...] = both[0]
    cg_ref[...] = both[1]
    outs = [
        pltpu.make_async_copy(bg_ref, bg_hbm, osem.at[0]),
        pltpu.make_async_copy(cg_ref, cg_hbm, osem.at[1]),
    ]
    for copy in outs:
        copy.start()
    for i, (lo, hi) in enumerate(CHUNKS):
        for copy in sums[i * (ways - 1) : (i + 1) * (ways - 1)]:
            copy.wait_recv()
        value = rs_send[tp, :, lo:hi].astype(F32)
        for k in range(ways - 1):
            value = value + rs_recv[k, :, lo:hi].astype(F32)
        out_ref[:, lo:hi] = value.astype(BF16)
    outs.append(pltpu.make_async_copy(out_ref, out_hbm, osem.at[2]))
    outs[2].start()

    for copy in gathers + bc_copies + sums:
        copy.wait_send()
    wait_sets(fy_buf, ys, yr, True)
    wait_sets(t_buf, ts, tr, True)
    for sem in (fs, ps, ss):
        wait_row(sem)
    for copy in outs:
        copy.wait()


def keep(*refs):
    count = len(refs) // 3
    results, outs, held = refs[:count], refs[count : 2 * count], refs[2 * count : 3 * count]
    sems = refs[-1]
    loads = [
        pltpu.make_async_copy(src, dst, sems.at[i]) for i, (src, dst) in enumerate(zip(results, held))
    ]
    stores = [
        pltpu.make_async_copy(src, dst, sems.at[count + i])
        for i, (src, dst) in enumerate(zip(held, outs))
    ]
    for copy in loads:
        copy.start()
    for load, store in zip(loads, stores):
        load.wait()
        store.start()
    for copy in stores:
        copy.wait()


def shards(
    layer_input,
    out_grad,
    w_in,
    w_gate,
    w_out,
    b_proj,
    c_proj,
    log_decay,
    d_skip,
    entry_state,
    doc_start,
):
    block, width = layer_input.shape
    channels = w_in.shape[0]
    state, tokens = b_proj.shape
    ways = lax.axis_size("tp")
    row_len = 8
    share = 2 * state // row_len
    groups = lax.axis_size("seq") // row_len
    tiles = -(-channels // LANES)
    anywhere = pl.BlockSpec(memory_space=pltpu.HBM)
    dma = pltpu.SemaphoreType.DMA
    results = pl.pallas_call(
        functools.partial(kernel, row_len, groups, SETS_Z, ways),
        out_shape=(
            jax.ShapeDtypeStruct((block, width), BF16),
            jax.ShapeDtypeStruct((state, tokens), F32),
            jax.ShapeDtypeStruct((state, tokens), F32),
        ),
        in_specs=[anywhere] * 11,
        out_specs=(anywhere, anywhere, anywhere),
        scratch_shapes=[
            pltpu.VMEM((ways, block, width), BF16),
            pltpu.VMEM((ways, block, width), BF16),
            pltpu.VMEM((channels, width), BF16),
            pltpu.VMEM((channels, width), BF16),
            pltpu.VMEM((channels, width), BF16),
            pltpu.VMEM(b_proj.shape, BF16),
            pltpu.VMEM(c_proj.shape, BF16),
            pltpu.VMEM(log_decay.shape, BF16),
            pltpu.VMEM((1, channels), F32),
            pltpu.VMEM(entry_state.shape, F32),
            pltpu.VMEM((1, tokens), jnp.int32),
            pltpu.VMEM((state // share, tiles * share, LANES), F32),
            pltpu.VMEM((tiles * share, LANES), F32),
            pltpu.VMEM((row_len, tiles * share, LANES), F32),
            pltpu.VMEM((row_len, tiles * share, LANES), F32),
            pltpu.VMEM((groups, tiles * share, LANES), F32),
            pltpu.VMEM((row_len, tiles * share, LANES), F32),
            pltpu.VMEM((row_len, tiles * share, LANES), F32),
            pltpu.VMEM((row_len, tiles * share, LANES), F32),
            pltpu.VMEM((row_len, tiles * share, LANES), F32),
            pltpu.VMEM((groups, tiles * share, LANES), F32),
            pltpu.VMEM((2, state, tiles * LANES), F32),
            pltpu.VMEM((ways, 2, state, tokens), F32),
            pltpu.VMEM((ways, block, width), BF16),
            pltpu.VMEM((ways - 1, block, width), BF16),
            pltpu.VMEM((block, width), BF16),
            pltpu.VMEM((state, tokens), F32),
            pltpu.VMEM((state, tokens), F32),
            dma((3,)),
            pltpu.SemaphoreType.REGULAR,
            dma((11,)),
            dma((2, 6)),
            dma((2, 6)),
            dma,
            dma,
            dma((groups,)),
            dma((groups,)),
            dma,
            dma,
            dma((groups,)),
            dma((groups,)),
            dma,
            dma,
            dma((ways - 1,)),
            dma((ways - 1,)),
            dma((len(CHUNKS), ways - 1)),
            dma((len(CHUNKS), ways - 1)),
        ],
        compiler_params=pltpu.CompilerParams(
            collective_id=0, has_side_effects=True, vmem_limit_bytes=64 * 1024 * 1024
        ),
        name="gated_recurrence_backward",
    )(
        layer_input,
        out_grad,
        w_in,
        w_gate,
        w_out,
        b_proj,
        c_proj,
        log_decay,
        d_skip.reshape(1, channels),
        entry_state,
        doc_start.reshape(1, tokens),
    )
    return pl.pallas_call(
        keep,
        out_shape=tuple(jax.ShapeDtypeStruct(r.shape, r.dtype) for r in results),
        in_specs=[anywhere] * 3,
        out_specs=(anywhere,) * 3,
        scratch_shapes=[pltpu.VMEM(r.shape, r.dtype) for r in results] + [dma((6,))],
        compiler_params=pltpu.CompilerParams(vmem_limit_bytes=64 * 1024 * 1024),
        name="results",
    )(*results)


def solution(mesh):
    in_specs = (
        P(("seq", "tp"), None),
        P(("seq", "tp"), None),
        P("tp", None),
        P("tp", None),
        P("tp", None),
        P(None, "seq"),
        P(None, "seq"),
        P(None, "seq"),
        P("tp"),
        P(None, "tp"),
        P("seq"),
    )
    out_specs = (P(("seq", "tp"), None), P(None, "seq"), P(None, "seq"))
    return jax.shard_map(shards, mesh=mesh, in_specs=in_specs, out_specs=out_specs, check_vma=False)
```

time: 73 us -> 53.6 us (0.73)
  local copies, waits for them, and re-layouts: 11.8 us -> 0 us
  Pallas kernels: 60.1 us -> 52.8 us
    unnamed x25 -> x0, local copies, waits for them, and re-layouts: 11.8 us -> none
    pallas_call x1 -> x2, Pallas kernels: 60.1 us -> 52.8 us  [the longest x1 51.2 us: shards(): pl.pallas_call(functools.partial(kernel, row_len, groups, SETS_Z, ways),...]
where the time goes in v2:
time: 53.6 us; the launch traced here: 53.4 us
  Pallas kernels  52.8 us (99%)
  between operations  0.64 us (1%)
    pallas_call x1, Pallas kernels, shards(): pl.pallas_call(functools.partial(kernel, row_len, groups, SETS_Z, ways),...  51.2 us
    pallas_call x1, Pallas kernels, shards(): pl.pallas_call(keep, out_shape=tuple((jax.ShapeDtypeStruct(r.shape, r.dty...  1.6 us

profile of v2, /device:TPU:1, one launch (start us, length us, event | category | flops | bytes accessed | tf_op | source)
XLA Modules:
  0.0 53.4 jit_solution(16834063328829660239)
XLA Ops:
  0.6 51.2 %gated_recurrence_backward.1 = (bf16[32,1600]{1,0:T(8,128)(2,1)}, f32[16,128]{1,0:T(8,128)}, f32[16,128]{1,0:T(8,128)}) custom-call(bf16[32,1600]{1,0:T(8,128)(2,1)} %x_hbm.1, bf16[32,1600]{1,0:T(8,128)(2,1)} %g_hbm.1, bf16[400,1600]{1,0:T(8,128)(2,1)} %wi_hbm.1, bf16[400,1600]{1,0:T(8,128)(2,1)} %wg_hbm.1, bf16[400,1600]{1,0:T(8,128)(2,1)} %wo_hbm.1, ...), custom_call_target="tpu_custom_call" | custom-call | tf_op jit(solution)/shard_map/gated_recurrence_backward/pallas_call | solution.py:565
  51.8 1.6 %results.1 = (bf16[32,1600]{1,0:T(8,128)(2,1)}, f32[16,128]{1,0:T(8,128)}, f32[16,128]{1,0:T(8,128)}) custom-call(bf16[32,1600]{1,0:T(8,128)(2,1)} %get-tuple-element.6.refs_0_, f32[16,128]{1,0:T(8,128)} %get-tuple-element.7.refs_1_, f32[16,128]{1,0:T(8,128)} %get-tuple-element.8.refs_2_), custom_call_target="tpu_custom_call" | custom-call | tf_op jit(solution)/shard_map/results/pallas_call | solution.py:640

commit v3 on v2

--- a/solution.py
+++ b/solution.py
@@ -63,9 +63,9 @@
     skip_hbm,
     entry_hbm,
     doc_hbm,
-    out_hbm,
-    bg_hbm,
-    cg_hbm,
+    out_ref,
+    bg_ref,
+    cg_ref,
     xbuf,
     gbuf,
     wi,
@@ -89,12 +89,9 @@
     t_buf,
     wide,
     bc_buf,
+    from_gate,
     rs_send,
     rs_recv,
-    out_ref,
-    bg_ref,
-    cg_ref,
-    osem,
     heard,
     lsem,
     gs,
@@ -260,6 +257,25 @@
 
         lax.fori_loop(1, row_len, send, 0)
 
+    def to_owners(side, src_at, dst, send_sem, recv_sem):
+        def send(i, carry):
+            peer = 2 * lax.rem(lax.div(rank, 2) + i, row_len // 2) + side
+
+            @pl.when(peer != rank)
+            def _():
+                pltpu.make_async_remote_copy(
+                    src_ref=src_at(peer),
+                    dst_ref=dst,
+                    send_sem=send_sem,
+                    recv_sem=recv_sem,
+                    device_id=(group * row_len + peer, tp),
+                    device_id_type=MESH,
+                ).start()
+
+            return carry
+
+        lax.fori_loop(0, row_len // 2, send, 0)
+
     def set_copy(buf, other, source, send_sem, recv_sem):
         return pltpu.make_async_remote_copy(
             src_ref=buf.at[source],
@@ -374,7 +390,7 @@
         f_pre[j] = product
         return product * f_recv[j]
 
-    fy_buf[group] = lax.fori_loop(0, row_len, decay_step, jnp.ones(f_send.shape, F32))
+    fy_buf[group] = lax.fori_loop(0, row_len, decay_step, jnp.ones(f_send.shape, F32), unroll=True)
 
     @pl.when(after > 0)
     def _():
@@ -396,6 +412,7 @@
     scaled_out = parts(scaled * carry_out, 2)
     state_part = mm((b_rows,), scaled_out, NN)
     lay_out(state_part, put_state)
+    to_owners(0, lambda peer: p_send.at[peer], p_recv.at[rank], ps, pr)
     gathered(1)
     local[4].wait()
     mix_grad = dot(gbuf[...].reshape(tokens, g_hbm.shape[1]), wo[...], NT)
@@ -404,8 +421,8 @@
     grad_part = mm((c_rows,), grads_in, NN)
     lay_out(grad_part, put_grad)
 
+    to_owners(1, lambda peer: p_send.at[peer], p_recv.at[rank], ps, pr)
     p_recv[rank] = p_send[rank]
-    to_row(lambda peer: p_send.at[peer], p_recv.at[rank], ps, pr)
 
     upper = parts(y_grads * rising, 2)
     lower = parts(scaled * falling, 2)
@@ -425,7 +442,7 @@
         res[j] = carried
         return f_recv[j] * carried + p_recv[j]
 
-    t_buf[group] = lax.fori_loop(0, row_len, scan_step, jnp.zeros(f_send.shape, F32))
+    t_buf[group] = lax.fori_loop(0, row_len, scan_step, jnp.zeros(f_send.shape, F32), unroll=True)
     to_sets(t_buf, ts, tr)
     wait_sets(fy_buf, ys, yr, False)
     wait_sets(t_buf, ts, tr, False)
@@ -436,36 +453,48 @@
         carried = jnp.where(i < ahead, fy_buf[j] * carried + t_buf[j], carried)
     res[...] = res[...] + f_pre[...] * carried[None]
     land[rank] = res[rank]
-    to_row(lambda peer: res.at[peer], land.at[rank], ss, sr)
-    wait_row(sr)
-
-    for q in range(state // share):
-        for k, lo, hi in spans:
-            for side in range(2):
+    to_row(lambda peer: res.at[peer], land.at[rank], ss, sr.at[rank])
+
+    def carried_in(side):
+        for q in range(state // share):
+            owner = 2 * q + side
+
+            @pl.when(owner != rank)
+            def _():
+                pltpu.make_async_copy(land.at[owner], land.at[owner], sr.at[owner]).wait()
+
+            for k, lo, hi in spans:
                 wide[side, share * q : share * (q + 1), lo : lo + LANES] = land[
-                    2 * q + side, share * k : share * (k + 1), :
+                    owner, share * k : share * (k + 1), :
                 ]
-    state_in = parts(wide[0, :, 0:channels], 2)
-    grad_in = parts(wide[1, :, 0:channels], 2)
+        return parts(wide[side, :, 0:channels], 2)
+
+    bc_copies = []
+
+    def share_out(side, value):
+        bc_buf[tp, side] = value
+        for k in range(1, ways):
+            copy = pltpu.make_async_remote_copy(
+                src_ref=bc_buf.at[tp, side],
+                dst_ref=bc_buf.at[tp, side],
+                send_sem=bs.at[side, k - 1],
+                recv_sem=br.at[side, k - 1],
+                device_id=(me, way_peer(k)),
+                device_id_type=MESH,
+            )
+            copy.start()
+            bc_copies.append(copy)
+
+    state_in = carried_in(0)
+    share_out(1, c_own + mm(state_in, grads_in, NT))
     ssm = (ssm_own + carry_in * mm((c_rows,), state_in, TN)).astype(BF16).astype(F32)
+    gate_grad = (ssm * gate_slope).astype(BF16)
+    from_gate[...] = dot(gate_grad, wg[...], NN)
+    grad_in = carried_in(1)
     x_part = x_own + carry_out * mm((b_rows,), grad_in, TN)
     x_grad = (x_part * scales + skip * y_grads).astype(BF16).astype(F32)
     pre_grad = (x_grad * pre_slope).astype(BF16)
-    gate_grad = (ssm * gate_slope).astype(BF16)
-    bc_buf[tp, 0] = b_own + mm(grad_in, scaled_out, NT)
-    bc_buf[tp, 1] = c_own + mm(state_in, grads_in, NT)
-    bc_copies = []
-    for k in range(1, ways):
-        copy = pltpu.make_async_remote_copy(
-            src_ref=bc_buf.at[tp],
-            dst_ref=bc_buf.at[tp],
-            send_sem=bs.at[k - 1],
-            recv_sem=br.at[k - 1],
-            device_id=(me, way_peer(k)),
-            device_id_type=MESH,
-        )
-        copy.start()
-        bc_copies.append(copy)
+    share_out(0, b_own + mm(grad_in, scaled_out, NT))
     order = (
         jnp.where(tp == 0, 3, jnp.where(tp == ways - 1, 1, 2)),
         jnp.where((tp == 0) | (tp == ways - 1), 2, 1),
@@ -473,7 +502,7 @@
     )
     sums = []
     for i, (lo, hi) in enumerate(CHUNKS):
-        part = dot(pre_grad, wi[:, lo:hi], NN) + dot(gate_grad, wg[:, lo:hi], NN)
+        part = dot(pre_grad, wi[:, lo:hi], NN) + from_gate[:, lo:hi]
         rs_send[:, :, lo:hi] = part.reshape(ways, block, hi - lo).astype(BF16)
         for k in order:
             copy = pltpu.make_async_remote_copy(
@@ -493,12 +522,6 @@
         both = both + bc_buf[k]
     bg_ref[...] = both[0]
     cg_ref[...] = both[1]
-    outs = [
-        pltpu.make_async_copy(bg_ref, bg_hbm, osem.at[0]),
-        pltpu.make_async_copy(cg_ref, cg_hbm, osem.at[1]),
-    ]
-    for copy in outs:
-        copy.start()
     for i, (lo, hi) in enumerate(CHUNKS):
         for copy in sums[i * (ways - 1) : (i + 1) * (ways - 1)]:
             copy.wait_recv()
@@ -506,8 +529,6 @@
         for k in range(ways - 1):
             value = value + rs_recv[k, :, lo:hi].astype(F32)
         out_ref[:, lo:hi] = value.astype(BF16)
-    outs.append(pltpu.make_async_copy(out_ref, out_hbm, osem.at[2]))
-    outs[2].start()
 
     for copy in gathers + bc_copies + sums:
         copy.wait_send()
@@ -515,27 +536,18 @@
     wait_sets(t_buf, ts, tr, True)
     for sem in (fs, ps, ss):
         wait_row(sem)
-    for copy in outs:
-        copy.wait()
 
 
 def keep(*refs):
-    count = len(refs) // 3
-    results, outs, held = refs[:count], refs[count : 2 * count], refs[2 * count : 3 * count]
+    half = len(refs) // 2
     sems = refs[-1]
-    loads = [
-        pltpu.make_async_copy(src, dst, sems.at[i]) for i, (src, dst) in enumerate(zip(results, held))
+    copies = [
+        pltpu.make_async_copy(src, dst, sems.at[i])
+        for i, (src, dst) in enumerate(zip(refs[:half], refs[half:-1]))
     ]
-    stores = [
-        pltpu.make_async_copy(src, dst, sems.at[count + i])
-        for i, (src, dst) in enumerate(zip(held, outs))
-    ]
-    for copy in loads:
+    for copy in copies:
         copy.start()
-    for load, store in zip(loads, stores):
-        load.wait()
-        store.start()
-    for copy in stores:
+    for copy in copies:
         copy.wait()
 
 
@@ -561,16 +573,17 @@
     groups = lax.axis_size("seq") // row_len
     tiles = -(-channels // LANES)
     anywhere = pl.BlockSpec(memory_space=pltpu.HBM)
+    inside = pl.BlockSpec(memory_space=pltpu.VMEM)
     dma = pltpu.SemaphoreType.DMA
     results = pl.pallas_call(
         functools.partial(kernel, row_len, groups, SETS_Z, ways),
         out_shape=(
-            jax.ShapeDtypeStruct((block, width), BF16),
-            jax.ShapeDtypeStruct((state, tokens), F32),
-            jax.ShapeDtypeStruct((state, tokens), F32),
+            pltpu.VMEM((block, width), BF16),
+            pltpu.VMEM((state, tokens), F32),
+            pltpu.VMEM((state, tokens), F32),
         ),
         in_specs=[anywhere] * 11,
-        out_specs=(anywhere, anywhere, anywhere),
+        out_specs=(inside, inside, inside),
         scratch_shapes=[
             pltpu.VMEM((ways, block, width), BF16),
             pltpu.VMEM((ways, block, width), BF16),
@@ -595,12 +608,9 @@
             pltpu.VMEM((groups, tiles * share, LANES), F32),
             pltpu.VMEM((2, state, tiles * LANES), F32),
             pltpu.VMEM((ways, 2, state, tokens), F32),
+            pltpu.VMEM((tokens, width), F32),
             pltpu.VMEM((ways, block, width), BF16),
             pltpu.VMEM((ways - 1, block, width), BF16),
-            pltpu.VMEM((block, width), BF16),
-            pltpu.VMEM((state, tokens), F32),
-            pltpu.VMEM((state, tokens), F32),
-            dma((3,)),
             pltpu.SemaphoreType.REGULAR,
             dma((11,)),
             dma((2, 6)),
@@ -614,36 +624,41 @@
             dma((groups,)),
             dma((groups,)),
             dma,
-            dma,
-            dma((ways - 1,)),
-            dma((ways - 1,)),
+            dma((row_len,)),
+            dma((2, ways - 1)),
+            dma((2, ways - 1)),
             dma((len(CHUNKS), ways - 1)),
             dma((len(CHUNKS), ways - 1)),
         ],
         compiler_params=pltpu.CompilerParams(
-            collective_id=0, has_side_effects=True, vmem_limit_bytes=64 * 1024 * 1024
+            collective_id=0, has_side_effects=True, vmem_limit_bytes=32 * 1024 * 1024
         ),
         name="gated_recurrence_backward",
     )(
-        layer_input,
-        out_grad,
-        w_in,
-        w_gate,
-        w_out,
-        b_proj,
-        c_proj,
-        log_decay,
-        d_skip.reshape(1, channels),
-        entry_state,
-        doc_start.reshape(1, tokens),
+        *(
+            pltpu.with_memory_space_constraint(value, pltpu.HBM)
+            for value in (
+                layer_input,
+                out_grad,
+                w_in,
+                w_gate,
+                w_out,
+                b_proj,
+                c_proj,
+                log_decay,
+                d_skip.reshape(1, channels),
+                entry_state,
+                doc_start.reshape(1, tokens),
+            )
+        )
     )
     return pl.pallas_call(
         keep,
         out_shape=tuple(jax.ShapeDtypeStruct(r.shape, r.dtype) for r in results),
-        in_specs=[anywhere] * 3,
+        in_specs=[inside] * 3,
         out_specs=(anywhere,) * 3,
-        scratch_shapes=[pltpu.VMEM(r.shape, r.dtype) for r in results] + [dma((6,))],
-        compiler_params=pltpu.CompilerParams(vmem_limit_bytes=64 * 1024 * 1024),
+        scratch_shapes=[dma((3,))],
+        compiler_params=pltpu.CompilerParams(vmem_limit_bytes=2 * 1024 * 1024),
         name="results",
     )(*results)
 

time: 53.6 us -> 51.3 us (0.957)
  Pallas kernels: 52.8 us -> 50.5 us
    pallas_call x1, Pallas kernels: 51.2 us -> 49.8 us  [shards(): pl.pallas_call(functools.partial(kernel, row_len, groups, SETS_Z, ways),...]
    pallas_call x1, Pallas kernels: 1.6 us -> 0.68 us  [shards(): pl.pallas_call(keep, out_shape=tuple((jax.ShapeDtypeStruct(r.shape, r.dty...]
where the time goes in v3:
time: 51.3 us; the launch traced here: 51.1 us
  Pallas kernels  50.5 us (98%)
  between operations  0.64 us (1%)
    pallas_call x1, Pallas kernels, shards(): pl.pallas_call(functools.partial(kernel, row_len, groups, SETS_Z, ways),...  49.8 us

profile of v3, /device:TPU:1, one launch (start us, length us, event | category | flops | bytes accessed | tf_op | source)
XLA Modules:
  0.0 51.1 jit_solution(9795507548231179185)
XLA Ops:
  0.6 49.8 %gated_recurrence_backward.1 = (bf16[32,1600]{1,0:T(8,128)(2,1)S(1)}, f32[16,128]{1,0:T(8,128)S(1)}, f32[16,128]{1,0:T(8,128)S(1)}) custom-call(bf16[32,1600]{1,0:T(8,128)(2,1)} %x_hbm.1, bf16[32,1600]{1,0:T(8,128)(2,1)} %g_hbm.1, bf16[400,1600]{1,0:T(8,128)(2,1)} %wi_hbm.1, bf16[400,1600]{1,0:T(8,128)(2,1)} %wg_hbm.1, bf16[400,1600]{1,0:T(8,128)(2,1)} %wo_hbm.1, ...), custom_call_target="tpu_custom_call" | custom-call | tf_op jit(solution)/shard_map/gated_recurrence_backward/pallas_call | solution.py:578
  50.5 0.7 %results.1 = (bf16[32,1600]{1,0:T(8,128)(2,1)}, f32[16,128]{1,0:T(8,128)}, f32[16,128]{1,0:T(8,128)}) custom-call(bf16[32,1600]{1,0:T(8,128)(2,1)S(1)} %get-tuple-element.6.refs_0_, f32[16,128]{1,0:T(8,128)S(1)} %get-tuple-element.7.refs_1_, f32[16,128]{1,0:T(8,128)S(1)} %get-tuple-element.8.refs_2_), custom_call_target="tpu_custom_call" | custom-call | tf_op jit(solution)/shard_map/results/pallas_call | solution.py:655

commit v4 on v3

--- a/solution.py
+++ b/solution.py
@@ -77,11 +77,13 @@
     skip_ref,
     entry_ref,
     doc_ref,
+    log_wide,
     entry_t,
     f_send,
     f_recv,
     f_pre,
     fy_buf,
+    fy_wide,
     p_send,
     p_recv,
     res,
@@ -156,7 +158,13 @@
 
     line, spot = lax.div(group, sets_z), lax.rem(group, sets_z)
     lines = groups // sets_z
-    last_line, last_spot = lines - 1 - line, sets_z - 1 - spot
+    last_line = lines - 1 - line
+
+    def turn_of(place):
+        return jnp.where(place < 2, place, 5 - place)
+
+    turn = turn_of(spot)
+    later = sets_z - 1 - turn
 
     def by_way(forward_value, backward_value):
         return forward_value * (1 - way) + backward_value * way
@@ -166,13 +174,26 @@
             other_spot, other_line = lax.div(i, lines), lax.rem(i, lines)
             other = other_line * sets_z + other_spot
             gap = (other - group) * (1 - 2 * way)
-            act(other, gap, other_spot)
+            act(other, gap, turn_of(other_spot))
             return carry
 
         lax.fori_loop(0, groups, step, 0)
 
+    def mirrored(place):
+        return row_len - 2 - place + 2 * lax.rem(place, 2)
+
+    def in_upper(place):
+        return place >= sets_z // 2
+
+    def share_of(member):
+        return jnp.where(in_upper(spot), mirrored(member), member)
+
+    mine = share_of(rank)
+
     def device_of(other):
-        return (other * row_len + rank, tp)
+        other_spot = lax.rem(other, sets_z)
+        across = in_upper(spot) != in_upper(other_spot)
+        return (other * row_len + jnp.where(across, mirrored(rank), rank), tp)
 
     barrier = pltpu.get_barrier_semaphore()
 
@@ -180,13 +201,13 @@
         pl.semaphore_signal(barrier, inc=1, device_id=(row_peer(i), tp), device_id_type=MESH)
         return carry
 
-    def greet_set(other, gap, other_spot):
-        @pl.when(((gap < 0) & (spot <= other_spot)) | ((gap > 0) & (spot < other_spot)))
+    def greet_set(other, gap, other_turn):
+        @pl.when(((gap < 0) & (turn <= other_turn)) | ((gap > 0) & (turn < other_turn)))
         def _():
             pl.semaphore_signal(barrier, inc=1, device_id=device_of(other), device_id_type=MESH)
 
-    def answer_set(other, gap, other_spot):
-        @pl.when((gap < 0) & (spot > other_spot))
+    def answer_set(other, gap, other_turn):
+        @pl.when((gap < 0) & (turn > other_turn))
         def _():
             pl.semaphore_signal(heard, inc=1, device_id=device_of(other), device_id_type=MESH)
 
@@ -194,11 +215,12 @@
         pl.semaphore_signal(barrier, inc=1, device_id=(me, way_peer(k)), device_id_type=MESH)
     lax.fori_loop(1, row_len, greet, 0)
     each_set(greet_set)
-    before = by_way(
-        last_line * (spot + 1) + (line + 1) * spot,
-        line * (spot + 1) + spot + last_line * spot,
+    before = by_way(last_line * (turn + 1) + line * turn, line * (turn + 1) + last_line * turn)
+    before = before + jnp.where(spot == 2, 1, 0) + jnp.minimum(spot, 2)
+    after = by_way(
+        last_line * later + jnp.where(spot < 2, 3 - spot, 0),
+        line * later + jnp.where(spot == 3, 1, 0),
     )
-    after = by_way((last_line + 1) * last_spot, line * last_spot)
     pl.semaphore_wait(barrier, row_len + ways - 2 + before)
 
     half = block // 2
@@ -235,12 +257,18 @@
         landed(array, way_peer(2), 0, 4)
         landed(array, way_peer(2), 1, 5)
 
-    for array in range(2):
+    def send_first(array):
         local[array].wait()
         pass_on(array, tp, 0, right, 0)
         pass_on(array, tp, 1, left, 3)
+
+    def send_second(array):
         pass_on(array, tp, 1, right, 1)
         pass_on(array, tp, 0, left, 2)
+
+    send_first(0)
+    send_second(0)
+    send_first(1)
     each_set(answer_set)
 
     def to_row(src_at, dst, send_sem, recv_sem):
@@ -287,7 +315,7 @@
         )
 
     def to_sets(buf, send_sem, recv_sem):
-        def send(other, gap, other_spot):
+        def send(other, gap, other_turn):
             @pl.when(gap > 0)
             def _():
                 set_copy(buf, other, group, send_sem, recv_sem).start()
@@ -295,7 +323,7 @@
         each_set(send)
 
     def wait_sets(buf, send_sem, recv_sem, sent):
-        def wait(other, gap, other_spot):
+        def wait(other, gap, other_turn):
             if sent:
 
                 @pl.when(gap > 0)
@@ -316,27 +344,35 @@
 
     for copy in small:
         copy.wait()
-    head_row = lax.broadcasted_iota(jnp.int32, (heads, channels), 0)
-    chan_row = lax.broadcasted_iota(jnp.int32, (heads, channels), 1) + tp * channels
+    rows_of = log_wide.shape[0]
+    head_row = lax.broadcasted_iota(jnp.int32, (rows_of, channels), 0)
+    chan_row = lax.broadcasted_iota(jnp.int32, (rows_of, channels), 1) + tp * channels
     low = head_row * HDIM
     pick = jnp.where((chan_row >= low) & (chan_row < low + HDIM), 1.0, 0.0).astype(BF16)
-    logs = dot(log_ref[...], pick, TN)
+    pick_all = jnp.concatenate([pick, pick, pick], axis=0)
+
+    def to_channels(value):
+        high = value.astype(BF16)
+        rest = value - high.astype(F32)
+        middle = rest.astype(BF16)
+        lowest = (rest - middle.astype(F32)).astype(BF16)
+        return dot(jnp.concatenate([high, middle, lowest], axis=0), pick_all, TN)
+
+    log_wide[...] = jnp.zeros_like(log_wide)
+    log_wide[0:heads, :] = log_ref[...].astype(F32)
+    logs = log_wide[...]
     row_at = lax.broadcasted_iota(jnp.int32, (tokens, tokens), 0)
     col_at = lax.broadcasted_iota(jnp.int32, (tokens, tokens), 1)
     tri = jnp.where(row_at >= col_at, 1.0, 0.0).astype(BF16)
-    eye = jnp.where(row_at == col_at, 1.0, 0.0).astype(BF16)
-    cumulative = dot(tri, logs.astype(BF16), NN)
     at = lax.broadcasted_iota(jnp.int32, (1, tokens), 1) + me
     marks = jnp.where(at > 0, doc_ref[...], 0).astype(F32)
-    marks_wide = jnp.broadcast_to(marks, (channels, tokens)).astype(BF16)
-    marks_sq = jnp.broadcast_to(marks, (tokens, tokens)).astype(BF16)
-    counts = dot(tri, marks_wide, NT)
-    mark_col = dot(eye, marks_wide, NT)
-    counts_col = dot(tri, marks_sq, NT)
-    counts_row = dot(marks_sq, tri, NT)
-    last = counts[tokens - 1 : tokens, :]
-    total = cumulative[tokens - 1 : tokens, :]
-    factor = jnp.where(last == 0.0, jnp.exp(total), 0.0)
+    marks_heads = jnp.broadcast_to(marks, logs.shape)
+    cumulative = dot(logs.astype(BF16), tri, NT)
+    counts = dot(marks_heads.astype(BF16), tri, NT)
+    last = counts[:, tokens - 1 : tokens]
+    total = cumulative[:, tokens - 1 : tokens]
+    carry_in = to_channels(jnp.where(counts == 0.0, jnp.exp(cumulative), 0.0))
+    factor = carry_in[tokens - 1 : tokens, :]
 
     f_send[...] = jnp.zeros_like(f_send)
     for k, lo, hi in spans:
@@ -346,6 +382,7 @@
     f_recv[rank] = f_send[...]
     to_row(lambda peer: f_send, f_recv.at[rank], fs, fr)
     forward(0)
+    send_second(1)
 
     p_send[...] = jnp.zeros_like(p_send)
     entry_t[...] = jnp.zeros_like(entry_t)
@@ -366,12 +403,16 @@
 
     lay_out(entry_ref[...], put_entry)
 
-    scales = jnp.where(mark_col == 1.0, 1.0, jnp.sqrt(one_minus_exp(-2.0 * logs)))
-    centre = cumulative[tokens // 2 : tokens // 2 + 1, :]
-    rising = jnp.exp(cumulative - centre)
-    falling = jnp.exp(centre - cumulative)
-    carry_in = jnp.where(counts == 0.0, jnp.exp(cumulative), 0.0)
-    carry_out = jnp.where(counts == last, jnp.exp(total - cumulative), 0.0)
+    scales = to_channels(
+        jnp.where(marks_heads == 1.0, 1.0, jnp.sqrt(one_minus_exp(-2.0 * logs)))
+    )
+    centre = cumulative[:, tokens // 2 : tokens // 2 + 1]
+    rising = to_channels(jnp.exp(cumulative - centre))
+    falling = to_channels(jnp.exp(centre - cumulative))
+    carry_out = to_channels(jnp.where(counts == last, jnp.exp(total - cumulative), 0.0))
+    marks_sq = jnp.broadcast_to(marks, (tokens, tokens)).astype(BF16)
+    counts_col = dot(tri, marks_sq, NT)
+    counts_row = dot(marks_sq, tri, NT)
     causal = (row_at >= col_at) & (counts_col == counts_row)
     b_rows = b_ref[...]
     c_rows = c_ref[...]
@@ -390,13 +431,14 @@
         f_pre[j] = product
         return product * f_recv[j]
 
-    fy_buf[group] = lax.fori_loop(0, row_len, decay_step, jnp.ones(f_send.shape, F32), unroll=True)
-
-    @pl.when(after > 0)
+    product = lax.fori_loop(0, row_len, decay_step, jnp.ones(f_send.shape, F32), unroll=True)
+    for k in range(tiles):
+        fy_buf[group, k : k + 1, :] = product[share * k : share * k + 1, :]
+
+    @pl.when(after == 0)
     def _():
-        pl.semaphore_wait(heard, after)
-
-    to_sets(fy_buf, ys, yr)
+        to_sets(fy_buf, ys, yr)
+
 
     gathered(0)
     local[2].wait()
@@ -412,7 +454,7 @@
     scaled_out = parts(scaled * carry_out, 2)
     state_part = mm((b_rows,), scaled_out, NN)
     lay_out(state_part, put_state)
-    to_owners(0, lambda peer: p_send.at[peer], p_recv.at[rank], ps, pr)
+    to_owners(0, lambda peer: p_send.at[share_of(peer)], p_recv.at[rank], ps, pr)
     gathered(1)
     local[4].wait()
     mix_grad = dot(gbuf[...].reshape(tokens, g_hbm.shape[1]), wo[...], NT)
@@ -421,8 +463,14 @@
     grad_part = mm((c_rows,), grads_in, NN)
     lay_out(grad_part, put_grad)
 
-    to_owners(1, lambda peer: p_send.at[peer], p_recv.at[rank], ps, pr)
-    p_recv[rank] = p_send[rank]
+    to_owners(1, lambda peer: p_send.at[share_of(peer)], p_recv.at[rank], ps, pr)
+    p_recv[rank] = p_send[mine]
+
+    @pl.when(after > 0)
+    def _():
+        pl.semaphore_wait(heard, after)
+        to_sets(fy_buf, ys, yr)
+
 
     upper = parts(y_grads * rising, 2)
     lower = parts(scaled * falling, 2)
@@ -445,21 +493,25 @@
     t_buf[group] = lax.fori_loop(0, row_len, scan_step, jnp.zeros(f_send.shape, F32), unroll=True)
     to_sets(t_buf, ts, tr)
     wait_sets(fy_buf, ys, yr, False)
+    for k in range(tiles):
+        fy_wide[:, share * k : share * (k + 1), :] = jnp.broadcast_to(
+            fy_buf[:, k : k + 1, :], (groups, share, LANES)
+        )
     wait_sets(t_buf, ts, tr, False)
-    carried = jnp.where(way == 0, entry_t[lax.div(rank, 2)], 0.0)
+    carried = jnp.where(way == 0, entry_t[lax.div(mine, 2)], 0.0)
     ahead = at_step(group, groups)
     for i in range(groups):
         j = at_step(i, groups)
-        carried = jnp.where(i < ahead, fy_buf[j] * carried + t_buf[j], carried)
+        carried = jnp.where(i < ahead, fy_wide[j] * carried + t_buf[j], carried)
     res[...] = res[...] + f_pre[...] * carried[None]
-    land[rank] = res[rank]
-    to_row(lambda peer: res.at[peer], land.at[rank], ss, sr.at[rank])
+    land[mine] = res[rank]
+    to_row(lambda peer: res.at[peer], land.at[mine], ss, sr.at[mine])
 
     def carried_in(side):
         for q in range(state // share):
             owner = 2 * q + side
 
-            @pl.when(owner != rank)
+            @pl.when(owner != mine)
             def _():
                 pltpu.make_async_copy(land.at[owner], land.at[owner], sr.at[owner]).wait()
 
@@ -494,7 +546,6 @@
     x_part = x_own + carry_out * mm((b_rows,), grad_in, TN)
     x_grad = (x_part * scales + skip * y_grads).astype(BF16).astype(F32)
     pre_grad = (x_grad * pre_slope).astype(BF16)
-    share_out(0, b_own + mm(grad_in, scaled_out, NT))
     order = (
         jnp.where(tp == 0, 3, jnp.where(tp == ways - 1, 1, 2)),
         jnp.where((tp == 0) | (tp == ways - 1), 2, 1),
@@ -515,6 +566,7 @@
             )
             copy.start()
             sums.append(copy)
+    share_out(0, b_own + mm(grad_in, scaled_out, NT))
     for copy in bc_copies:
         copy.wait_recv()
     both = bc_buf[0]
@@ -596,10 +648,12 @@
             pltpu.VMEM((1, channels), F32),
             pltpu.VMEM(entry_state.shape, F32),
             pltpu.VMEM((1, tokens), jnp.int32),
+            pltpu.VMEM((-(-log_decay.shape[0] // 16) * 16, tokens), F32),
             pltpu.VMEM((state // share, tiles * share, LANES), F32),
             pltpu.VMEM((tiles * share, LANES), F32),
             pltpu.VMEM((row_len, tiles * share, LANES), F32),
             pltpu.VMEM((row_len, tiles * share, LANES), F32),
+            pltpu.VMEM((groups, tiles, LANES), F32),
             pltpu.VMEM((groups, tiles * share, LANES), F32),
             pltpu.VMEM((row_len, tiles * share, LANES), F32),
             pltpu.VMEM((row_len, tiles * share, LANES), F32),

time: 51.3 us -> 50.6 us (0.986)
  Pallas kernels: 50.5 us -> 49.8 us
    pallas_call x1, Pallas kernels: 49.8 us -> 49.1 us  [shards(): pl.pallas_call(functools.partial(kernel, row_len, groups, SETS_Z, ways),...]
where the time goes in v4:
time: 50.6 us; the launch traced here: 50.5 us
  Pallas kernels  49.8 us (98%)
  between operations  0.64 us (1%)
    pallas_call x1, Pallas kernels, shards(): pl.pallas_call(functools.partial(kernel, row_len, groups, SETS_Z, ways),...  49.1 us

profile of v4, /device:TPU:1, one launch (start us, length us, event | category | flops | bytes accessed | tf_op | source)
XLA Modules:
  0.0 50.5 jit_solution(18121531818162434053)
XLA Ops:
  0.6 49.1 %gated_recurrence_backward.1 = (bf16[32,1600]{1,0:T(8,128)(2,1)S(1)}, f32[16,128]{1,0:T(8,128)S(1)}, f32[16,128]{1,0:T(8,128)S(1)}) custom-call(bf16[32,1600]{1,0:T(8,128)(2,1)} %x_hbm.1, bf16[32,1600]{1,0:T(8,128)(2,1)} %g_hbm.1, bf16[400,1600]{1,0:T(8,128)(2,1)} %wi_hbm.1, bf16[400,1600]{1,0:T(8,128)(2,1)} %wg_hbm.1, bf16[400,1600]{1,0:T(8,128)(2,1)} %wo_hbm.1, ...), custom_call_target="tpu_custom_call" | custom-call | tf_op jit(solution)/shard_map/gated_recurrence_backward/pallas_call | solution.py:630
  49.8 0.7 %results.1 = (bf16[32,1600]{1,0:T(8,128)(2,1)}, f32[16,128]{1,0:T(8,128)}, f32[16,128]{1,0:T(8,128)}) custom-call(bf16[32,1600]{1,0:T(8,128)(2,1)S(1)} %get-tuple-element.6.refs_0_, f32[16,128]{1,0:T(8,128)S(1)} %get-tuple-element.7.refs_1_, f32[16,128]{1,0:T(8,128)S(1)} %get-tuple-element.8.refs_2_), custom_call_target="tpu_custom_call" | custom-call | tf_op jit(solution)/shard_map/results/pallas_call | solution.py:709

commit v5 on v4

--- a/solution.py
+++ b/solution.py
@@ -177,7 +177,7 @@
             act(other, gap, turn_of(other_spot))
             return carry
 
-        lax.fori_loop(0, groups, step, 0)
+        lax.fori_loop(0, groups, step, 0, unroll=True)
 
     def mirrored(place):
         return row_len - 2 - place + 2 * lax.rem(place, 2)

time: 50.6 us -> 50.5 us (level)
  no operation moved by 1% of the time
where the time goes in v5:
time: 50.5 us; the launch traced here: 50.4 us
  Pallas kernels  49.7 us (98%)
  between operations  0.64 us (1%)
    pallas_call x1, Pallas kernels, shards(): pl.pallas_call(functools.partial(kernel, row_len, groups, SETS_Z, ways),...  49 us

profile of v5, /device:TPU:1, one launch (start us, length us, event | category | flops | bytes accessed | tf_op | source)
XLA Modules:
  0.0 50.4 jit_solution(8138313829516394440)
XLA Ops:
  0.6 49.0 %gated_recurrence_backward.1 = (bf16[32,1600]{1,0:T(8,128)(2,1)S(1)}, f32[16,128]{1,0:T(8,128)S(1)}, f32[16,128]{1,0:T(8,128)S(1)}) custom-call(bf16[32,1600]{1,0:T(8,128)(2,1)} %x_hbm.1, bf16[32,1600]{1,0:T(8,128)(2,1)} %g_hbm.1, bf16[400,1600]{1,0:T(8,128)(2,1)} %wi_hbm.1, bf16[400,1600]{1,0:T(8,128)(2,1)} %wg_hbm.1, bf16[400,1600]{1,0:T(8,128)(2,1)} %wo_hbm.1, ...), custom_call_target="tpu_custom_call" | custom-call | tf_op jit(solution)/shard_map/gated_recurrence_backward/pallas_call | solution.py:630
  49.7 0.7 %results.1 = (bf16[32,1600]{1,0:T(8,128)(2,1)}, f32[16,128]{1,0:T(8,128)}, f32[16,128]{1,0:T(8,128)}) custom-call(bf16[32,1600]{1,0:T(8,128)(2,1)S(1)} %get-tuple-element.6.refs_0_, f32[16,128]{1,0:T(8,128)S(1)} %get-tuple-element.7.refs_1_, f32[16,128]{1,0:T(8,128)S(1)} %get-tuple-element.8.refs_2_), custom_call_target="tpu_custom_call" | custom-call | tf_op jit(solution)/shard_map/results/pallas_call | solution.py:709
